TPU v7x, 32 devices: a whole 2x2x4 slice. The times are simulated.
32 devices in a mesh: lat: 16 (over z, x, core), lon: 2 (over y).
Axes of the slice: x: 2, y: 2, z: 4, core: 2. Of those that a mesh axis runs over, the one named last changes fastest.
Arguments:
- clean: float32 [4, 256, 256], P(None, 'lat', 'lon'), may hold values from -6 to 6
- noise: float32 [4, 256, 256], P(None, 'lat', 'lon'), may hold values from -6 to 6
- mean_field: float32 [4, 256, 256], P(None, 'lat', 'lon'), may hold values from -6 to 6
- sigma_index: int32 [1], replicated, may hold values from 0 to 15
- teacher_lift: bfloat16 [128, 8], replicated, may hold values from -2 to 2
- teacher_first: bfloat16 [128, 9, 128], replicated, may hold values from -0.1875 to 0.1875
- teacher_second: bfloat16 [128, 9, 128], replicated, may hold values from -0.1875 to 0.1875
- teacher_proj: bfloat16 [4, 128], replicated, may hold values from -0.5 to 0.5
- student_lift: bfloat16 [128, 8], replicated, may hold values from -2 to 2
- student_first: bfloat16 [128, 9, 128], replicated, may hold values from -0.1875 to 0.1875
- student_second: bfloat16 [128, 9, 128], replicated, may hold values from -0.1875 to 0.1875
- student_proj: bfloat16 [4, 128], replicated, may hold values from -0.5 to 0.5
Outputs:
- target: float32 [4, 256, 256], P(None, 'lat', 'lon')
- update_first: float32 [128, 9, 128], replicated
- update_second: float32 [128, 9, 128], replicated
All inputs are finite; a program needn't handle non-finite values.
Results may differ from a plain program's by a relative error of at most 0.0038.
Values may be sent and summed in bfloat16 or wider, within the bound.
A program may use at most 128 MiB of HBM per device.

v0:
```python
import functools

import jax
import jax.numpy as jnp
import numpy as np
from jax import lax
from jax.experimental import pallas as pl
from jax.experimental.pallas import tpu as pltpu
from jax.sharding import PartitionSpec as P

SCHED = 18
HALO = 9
SIDE = 16
C = 128
F32 = jnp.float32
BF16 = jnp.bfloat16

LANE = np.arange(128)
LANE_A, LANE_J, LANE_CH = LANE // 32, LANE % 32 // 8, LANE % 8
LANE_SIDE = np.array([1, 0, 1, 0])[LANE_J]


def plan_sigma(index):
    steps = jnp.arange(SCHED, dtype=jnp.int32)
    ramp = steps.astype(F32) / (SCHED - 1)
    top = 80.0 ** (1.0 / 7.0)
    bottom = 0.02 ** (1.0 / 7.0)
    table = (top + ramp * (bottom - top)) ** 7.0
    return jnp.sum(jnp.where(steps == index, table, jnp.zeros_like(table)))


def silu(v):
    u = 0.5 * v
    return u + u * jnp.tanh(u)


def silu_slope(v):
    sig = 0.5 + 0.5 * jnp.tanh(0.5 * v)
    return sig * (1.0 + v * (1.0 - sig))


def kernel(
    rows, pairs, center,
    sc, edge, xin, sel, t_w1, t_w2, t_pr, s_w1, s_w2, s_pr, s_r, s_pt,
    tgt_ref, g2_ref, g1_ref,
    x0, xa, xb, fld, u2, x4, dz4, slope1, slope2, dpre,
):
    total = rows + 2 * HALO
    top = edge[0] == 1
    bottom = edge[1] == 1
    lane = lax.broadcasted_iota(jnp.int32, (1, 1, 128), 2)
    lane_a = lane // 32
    lane_j = lane % 32 // 8
    is_x = lane % 8 < 4

    def zero_edges(ref):
        @pl.when(top)
        def _():
            ref[0:HALO] = jnp.zeros((HALO,) + ref.shape[1:], ref.dtype)

        @pl.when(bottom)
        def _():
            ref[HALO + rows : total] = jnp.zeros((HALO,) + ref.shape[1:], ref.dtype)

    def blocks(first, last, size, body):
        count = -(-(last - first) // size)

        def step(i, carry):
            body(jnp.minimum(first + i * size, last - size))
            return carry

        lax.fori_loop(0, count, step, 0)

    def load_state(r):
        part = xin[pl.ds(r, 2)].reshape(2 * pairs, 16)
        x0[pl.ds(r, 2)] = jnp.dot(
            part, sel[...], precision=lax.Precision.HIGHEST, preferred_element_type=F32
        ).reshape(2, pairs, 128)

    blocks(0, total, 2, load_state)

    def spread(value, ref, r, nb):
        for n in range(nb):
            row = value[n]
            ref[r + n, :, 0:128] = pltpu.roll(row[:, 128:], 1, 0).astype(BF16)
            ref[r + n, :, 128:384] = row.astype(BF16)
            ref[r + n, :, 384:512] = pltpu.roll(row[:, :128], pairs - 1, 0).astype(BF16)

    def conv1(state, q_inv, w1, first, last, nb, save):
        scale = jnp.where(is_x, q_inv, 1.0)

        def body(r):
            xs = state[pl.ds(r - 1, nb + 2)] * scale
            shifted = []
            for n in range(nb + 2):
                row = xs[n]
                back = pltpu.roll(row, 1, 0)
                ahead = pltpu.roll(row, pairs - 1, 0)
                shifted.append(jnp.where(lane_j[0] == 0, back, jnp.where(lane_j[0] == 3, ahead, row)))
            u = jnp.stack(
                [
                    jnp.where(
                        lane_a[0] == 0,
                        shifted[n],
                        jnp.where(lane_a[0] == 1, shifted[n + 1], shifted[n + 2]),
                    )
                    for n in range(nb)
                ]
            ).astype(BF16)
            u2[pl.ds(r, nb)] = u
            flat = u.reshape(nb * pairs, 128)
            pre = jnp.dot(
                jnp.concatenate([flat, flat], axis=1), w1[...], preferred_element_type=F32
            ).reshape(nb, pairs, 256)
            spread(silu(pre), x4, r, nb)
            if save:
                slope1[pl.ds(r, nb)] = silu_slope(pre)

        blocks(first, last, nb, body)
        zero_edges(x4)

    def conv2(w2, pr, first, last, nb, save):
        def body(r):
            lhs = jnp.concatenate(
                [x4[pl.ds(r + a - 1, nb)].reshape(nb * pairs, 512) for a in range(3)]
                + [u2[pl.ds(r, nb)].reshape(nb * pairs, 128)],
                axis=1,
            )
            z = jnp.dot(lhs, w2[...], preferred_element_type=F32)
            g = silu(z).astype(BF16)
            fld[pl.ds(r, nb)] = jnp.dot(g, pr[...], preferred_element_type=F32).reshape(
                nb, pairs, 128
            )
            if save:
                slope2[pl.ds(r, nb)] = silu_slope(z).reshape(nb, pairs, 256)

        blocks(first, last, nb, body)
        zero_edges(fld)

    s0, s1, s2 = sc[0], sc[1], sc[2]
    q_inv = [sc[3], sc[4], sc[5]]
    rest = [sc[6], sc[7], sc[8]]
    keep = [sc[9], sc[10], sc[11]]
    gain = [sc[12], sc[13], sc[14]]
    h0, h1 = sc[15], sc[16]
    h0_a, h0_b, h1_b, h1_c = sc[17], sc[18], sc[19], sc[20]
    back = sc[21]
    pull = sc[22]

    def teacher(state, level, first):
        last = total - first
        conv1(state, q_inv[level], t_w1, first, last, 4, False)
        conv2(t_w2, t_pr, first + 1, last - 1, 6, False)

    def update(dst, first, fn):
        def body(r):
            at = pl.ds(r, 2)
            dst[at] = fn(at)

        blocks(first, total - first, 2, body)

    def euler(src, dst, first, level, ratio):
        cx = jnp.where(is_x, 1.0 + ratio * rest[level], 1.0)
        cf = ratio * gain[level]
        update(dst, first, lambda at: src[at] * cx - fld[at] * cf)

    def correct(src, guess, dst, first, level, ratio):
        cx = jnp.where(is_x, 0.5 + 0.5 * ratio * rest[level], 0.5)
        cf = 0.5 * ratio * gain[level]
        update(dst, first, lambda at: 0.5 * src[at] + guess[at] * cx - fld[at] * cf)

    teacher(x0, 0, 1)
    euler(x0, xa, 2, 0, h0_a)
    teacher(xa, 1, 3)
    correct(x0, xa, xb, 4, 1, h0_b)
    teacher(xb, 1, 5)
    euler(xb, xa, 6, 1, h1_b)
    teacher(xa, 2, 7)
    correct(xb, xa, xb, 8, 2, h1_c)

    def make_target(at):
        start = x0[at]
        return start - (xb[at] - start) * back

    update(xa, 8, make_target)
    tgt_ref[...] = xa[HALO : HALO + rows, 0:center, :]

    conv1(x0, q_inv[0], s_w1, 7, total - 7, 4, True)
    conv2(s_w2, s_pr, 8, total - 8, 6, True)

    def backward(r):
        at = pl.ds(r, 2)
        d_field = jnp.where(
            is_x, pull * (keep[0] * x0[at] + gain[0] * fld[at] - xa[at]), 0.0
        ).astype(BF16)
        d_gated = jnp.dot(
            d_field.reshape(2 * pairs, 128), s_pt[...], preferred_element_type=F32
        ).reshape(2, pairs, 256)
        spread(d_gated * slope2[at], dz4, r, 2)

    blocks(8, total - 8, 2, backward)
    zero_edges(dz4)

    cells = rows * center
    dims = (((0,), (0,)), ((), ()))
    middle = pl.ds(HALO, rows)
    dz = dz4[middle, 0:center, 128:384].reshape(cells, 256)
    for a in range(3):
        near = x4[pl.ds(HALO - 1 + a, rows), 0:center, :].reshape(cells, 512)
        grad = lax.dot_general(dz, near, dims, preferred_element_type=F32)
        g2_ref[:, a * 384 : (a + 1) * 384] = grad[:128, 0:384] + grad[128:, 128:512]

    def conv3(r):
        lhs = jnp.concatenate(
            [dz4[pl.ds(r + a - 1, 4)].reshape(4 * pairs, 512) for a in range(3)], axis=1
        )
        dh = jnp.dot(lhs, s_r[...], preferred_element_type=F32).reshape(4, pairs, 256)
        dpre[pl.ds(r - HALO, 4)] = (dh * slope1[pl.ds(r, 4)]).astype(BF16)

    blocks(HALO, HALO + rows, 4, conv3)
    d_before = dpre[:, 0:center, :].reshape(cells, 256)
    near = u2[middle, 0:center, :].reshape(cells, 128)
    grad = lax.dot_general(d_before, near, dims, preferred_element_type=F32)
    g1_ref[...] = grad[:128] + pltpu.roll(grad[128:], 120, 1)


def pair_weights(taps):
    none = jnp.zeros_like(taps[:, :1])
    even = jnp.concatenate([taps, none], axis=1)
    odd = jnp.concatenate([none, taps], axis=1)
    both = jnp.concatenate([even, odd], axis=3)
    return both.reshape(12 * taps.shape[2], 2 * taps.shape[3])


def second_weights(second, lift):
    taps = second.reshape(C, 3, 3, C).transpose(1, 2, 3, 0)
    lift_t = lift.T
    none = jnp.zeros((8, C), lift.dtype)
    center = jnp.concatenate(
        [
            jnp.zeros((40, 2 * C), lift.dtype),
            jnp.concatenate([lift_t, none], axis=1),
            jnp.concatenate([none, lift_t], axis=1),
            jnp.zeros((72, 2 * C), lift.dtype),
        ],
        axis=0,
    )
    return jnp.concatenate([pair_weights(taps), center], axis=0)


def first_weights(first, lift):
    joined = jnp.einsum("oti,ic->tco", first, lift, preferred_element_type=F32)
    full = pair_weights(joined.reshape(3, 3, 8, C))
    full = jnp.pad(full, ((0, 32), (0, 0)))
    high = lax.reduce_precision(full, 8, 7)
    return jnp.concatenate([high, full - high], axis=0).astype(BF16)


def proj_weights(proj):
    spot = (LANE_CH < 4) & (LANE < 96)
    wide = jnp.where(spot[None, :], proj.T[:, LANE_CH % 4], 0)
    even = jnp.where((LANE_SIDE == 0)[None, :], wide, 0)
    odd = jnp.where((LANE_SIDE == 1)[None, :], wide, 0)
    return jnp.concatenate([even, odd], axis=0).astype(BF16)


def back_weights(proj):
    four = jnp.concatenate([proj, jnp.zeros_like(proj)], axis=0)
    none = jnp.zeros_like(four)
    return jnp.concatenate(
        [
            jnp.zeros((40, 2 * C), proj.dtype),
            jnp.concatenate([four, none], axis=1),
            jnp.concatenate([none, four], axis=1),
            jnp.zeros((72, 2 * C), proj.dtype),
        ],
        axis=0,
    )


def local(
    clean, noise, mean_field, sigma_index,
    teacher_lift, teacher_first, teacher_second, teacher_proj,
    student_lift, student_first, student_second, student_proj,
):
    start = sigma_index[0]
    s0, s1, s2 = plan_sigma(start), plan_sigma(start + 1), plan_sigma(start + 2)
    sig = jnp.stack([s0, s1, s2])
    q2 = sig * sig + 0.25
    q = jnp.sqrt(q2)
    weight = q2[0] / (s0 * s0 * 0.25)
    h0, h1 = s1 - s0, s2 - s1
    scalars = jnp.concatenate(
        [
            sig, 1.0 / q, sig * sig / q2, 0.25 / q2, sig * 0.5 / q,
            jnp.stack(
                [h0, h1, h0 / s0, h0 / s1, h1 / s1, h1 / s2, s0 / (s2 - s0),
                 s0 * 0.5 / q[0] * 2.0 * weight]
            ),
        ]
    )
    rows, cols = clean.shape[1:]
    lat, lon = lax.axis_size("lat"), lax.axis_size("lon")
    me = lax.axis_index("lat")
    edge = jnp.stack([me == 0, me == lat - 1]).astype(jnp.int32)

    cells = jnp.concatenate([clean + s0 * noise, mean_field], axis=0)
    ring = [(i, (i + 1) % lon) for i in range(lon)]
    left = lax.ppermute(cells[:, :, cols - SIDE :], "lon", ring)
    right = lax.ppermute(cells[:, :, :SIDE], "lon", [(b, a) for a, b in ring])
    cells = jnp.concatenate([cells, right, left], axis=2)
    up = [(i, i + 1) for i in range(lat - 1)]
    above = lax.ppermute(cells[:, rows - HALO :], "lat", up)
    below = lax.ppermute(cells[:, :HALO], "lat", [(b, a) for a, b in up])
    cells = jnp.concatenate([above, cells, below], axis=1)
    total, pairs, center = rows + 2 * HALO, (cols + 2 * SIDE) // 2, cols // 2
    xin = cells.reshape(8, total, pairs, 2).transpose(1, 2, 3, 0).reshape(total, pairs, 16)

    sel = (
        (np.arange(16)[:, None] == (LANE_SIDE * 8 + LANE_CH)[None, :]) & (LANE < 96)[None, :]
    ).astype(np.float32)
    back = student_second[:, ::-1, :].reshape(C, 3, 3, C).transpose(1, 2, 0, 3)
    operands = [
        scalars, edge, xin, jnp.asarray(sel),
        first_weights(teacher_first, teacher_lift),
        second_weights(teacher_second, teacher_lift),
        proj_weights(teacher_proj),
        first_weights(student_first, student_lift),
        second_weights(student_second, student_lift),
        proj_weights(student_proj),
        pair_weights(back),
        back_weights(student_proj),
    ]
    vmem = pl.BlockSpec(memory_space=pltpu.VMEM)
    smem = pl.BlockSpec(memory_space=pltpu.SMEM)
    tgt, g2, g1 = pl.pallas_call(
        functools.partial(kernel, rows, pairs, center),
        out_shape=[
            jax.ShapeDtypeStruct((rows, center, 128), F32),
            jax.ShapeDtypeStruct((C, 9 * C), F32),
            jax.ShapeDtypeStruct((C, 128), F32),
        ],
        in_specs=[smem, smem] + [vmem] * 10,
        out_specs=[vmem] * 3,
        scratch_shapes=[pltpu.VMEM((total, pairs, 128), F32)] * 4
        + [
            pltpu.VMEM((total, pairs, 128), BF16),
            pltpu.VMEM((total, pairs, 512), BF16),
            pltpu.VMEM((total, pairs, 512), BF16),
            pltpu.VMEM((total, pairs, 256), F32),
            pltpu.VMEM((total, pairs, 256), F32),
            pltpu.VMEM((rows, pairs, 256), BF16),
        ],
        compiler_params=pltpu.CompilerParams(vmem_limit_bytes=56 * 1024 * 1024),
    )(*operands)
    target = (
        tgt[:, :, 8:24].reshape(rows, center, 2, 8)[..., :4].transpose(3, 0, 1, 2)
    ).reshape(4, rows, cols)
    g2, g1 = lax.psum((g2, g1), ("lat", "lon"))
    spots = g1[:, :96].reshape(C, 3, 4, 8)[:, :, :3].reshape(C, 9, 8)
    grad_first = jnp.einsum(
        "otc,ic->oti", spots, student_lift.astype(F32), precision=lax.Precision.HIGHEST
    )
    update_first = grad_first * lax.rsqrt(jnp.mean(grad_first * grad_first) + 1e-06)
    update_second = g2 * lax.rsqrt(jnp.mean(g2 * g2) + 1e-06)
    return (target, update_first, update_second.reshape(C, 9, C))


def solution(mesh):
    grid = P(None, "lat", "lon")
    return jax.shard_map(
        local,
        mesh=mesh,
        in_specs=(grid, grid, grid) + (P(),) * 9,
        out_specs=(grid, P(), P()),
        check_vma=False,
    )
```

profile of v0, /device:TPU:0, one launch (start us, length us, event | category | flops | bytes accessed | tf_op | source)
XLA Modules:
  0.0 229.4 jit_solution(9962570477765716850)
XLA Ops:
  8.6 1.4 multiply_add_fusion
  10.0 0.9 slice_maximum_fusion
  10.9 3.0 %collective-permute-start = (f32[8,16,16]{2,1,0:T(8,128)S(1)}, f32[8,16,16]{2,1,0:T(8,128)S(1)}, u32[]{:S(2)}, u32[]{:S(2)}) collective-permute-start(f32[8,16,16]{2,1,0:T(8,128)S(1)} %get-tuple-element.25), channel_id=1, source_target_pairs={{1,0},{0,1},{3,2},{2,3},{5,4},{4,5},{7,6},{6,7},{9,8},{8,9},{11,10... | collective-permute-start | bytes 24584 | tf_op jit(solution)/shard_map/ppermute | solution.py:310
  14.6 2.0 multiply_add_fusion.1
  16.7 0.7 pad_clamp_fusion
  17.3 0.7 concatenate.131
  18.0 1.3 gather_fusion.1
  19.5 1.3 gather_fusion
  21.0 0.9 fusion.20
  22.6 1.0 fusion.8
  24.5 0.8 pad_maximum_fusion.2
  26.8 1.5 collective-permute-start.2
  28.3 1.3 collective-permute-start.3
  39.5 2.5 %concatenate.102.sc = f32[23]{0:T(128)} concatenate(f32[1]{0:T(128)} %bitcast.1, f32[1]{0:T(128)} %bitcast.2, f32[1]{0:T(128)} %bitcast.3, f32[3]{0:T(128)S(1)} %get-tuple-element.35, f32[3]{0:T(128)S(1)} %get-tuple-element.36, f32[3]{0:T(128)S(1)} %get-tuple-element.34, f32[3]{0:T(128)S(1)} %get-tuple-element.37, f32[1]{0:T(128)} %bitcast.4, f32[1]{0:T(128)} %bitcast.5, ...), dimensions={0} | concatenate | bytes 184 | tf_op jit(solution)/shard_map/concatenate | solution.py:293
  42.5 1.7 copy.40.xin
  44.2 37.4 %shard_map.238 = (f32[16,64,128]{2,1,0:T(8,128)}, f32[128,1152]{1,0:T(8,128)}, f32[128,128]{1,0:T(8,128)}) custom-call(f32[23]{0:T(128)} %concatenate.102.sc, s32[2]{0:T(128)} %add_convert_fusion.edge, f32[34,80,16]{2,1,0:T(8,128)} %copy.40.xin, f32[16,128]{1,0:T(8,128)} %constant.23.clone.sel, bf16[256,256]{1,0:T(8,128)(2,1)} %get-tuple-element.44.t_w1, ...), custom_call_target="tpu_custom_call" | custom-call | tf_op jit(solution)/shard_map/pallas_call | solution.py:336
  81.6 1.2 slice.36
  83.2 0.7 copy.45
  83.9 130.9 %all-reduce.22.cloned.1.call-done = (f32[128,128]{1,0:T(8,128)}, f32[128,1152]{1,0:T(8,128)}) async-done(((f32[128,128]{1,0:T(8,128)}, f32[128,1152]{1,0:T(8,128)}), (f32[128,128]{1,0:T(8,128)}, f32[128,1152]{1,0:T(8,128)})) %all-reduce.22.cloned.1.call-update) | async-done | bytes 655376 | tf_op jit(solution)/shard_map/psum | solution.py:359
  214.8 1.9 multiply_reduce_fusion
  217.4 0.9 copy.43
  218.4 1.3 multiply_reduce_fusion.1
  220.6 1.1 copy.46
  221.7 0.9 broadcast_multiply_fusion.1
  (73 shorter events, 6.2 us)
Async XLA Ops:
  7.2 13.8 %copy-start = (bf16[128,9,128]{2,0,1:T(8,128)(2,1)S(1)}, bf16[128,9,128]{2,0,1:T(8,128)(2,1)}, u32[]{:S(2)}) copy-start(bf16[128,9,128]{2,0,1:T(8,128)(2,1)} %param.32) | copy-start | bytes 884740
  7.2 14.7 %copy-start.9 = (bf16[128,8]{0,1:T(8,128)(2,1)S(1)}, bf16[128,8]{0,1:T(8,128)(2,1)}, u32[]{:S(2)}) copy-start(bf16[128,8]{0,1:T(8,128)(2,1)} %param.27) | copy-start | bytes 6148
  7.2 14.7 %copy-start.7 = (bf16[128,9,128]{2,0,1:T(8,128)(2,1)S(1)}, bf16[128,9,128]{2,0,1:T(8,128)(2,1)}, u32[]{:S(2)}) copy-start(bf16[128,9,128]{2,0,1:T(8,128)(2,1)} %param.28) | copy-start | bytes 884740
  7.2 15.0 %copy-start.6 = (bf16[128,9,128]{2,0,1:T(8,128)(2,1)S(1)}, bf16[128,9,128]{2,0,1:T(8,128)(2,1)}, u32[]{:S(2)}) copy-start(bf16[128,9,128]{2,0,1:T(8,128)(2,1)} %param.29) | copy-start | bytes 884740
  7.2 207.6 %all-reduce.22.cloned.1.call-start = ((), (), s32[]{:S(2)}) async-start(), calls=%async_computation | async-start | bytes 1310720 | tf_op jit(solution)/shard_map/psum | solution.py:359
  10.9 11.5 %copy-start.4 = (bf16[128,9,128]{2,0,1:T(8,128)(2,1)S(1)}, bf16[128,9,128]{2,0,1:T(8,128)(2,1)}, u32[]{:S(2)}) copy-start(bf16[128,9,128]{2,0,1:T(8,128)(2,1)} %param.33) | copy-start | bytes 884740
  10.9 15.7 %collective-permute-start = (f32[8,16,16]{2,1,0:T(8,128)S(1)}, f32[8,16,16]{2,1,0:T(8,128)S(1)}, u32[]{:S(2)}, u32[]{:S(2)}) collective-permute-start(f32[8,16,16]{2,1,0:T(8,128)S(1)} %get-tuple-element.25), channel_id=1, source_target_pairs={{1,0},{0,1},{3,2},{2,3},{5,4},{4,5},{7,6},{6,7},{9,8},{8,9},{11,10... | collective-permute-start | bytes 24584 | tf_op jit(solution)/shard_map/ppermute | solution.py:310
  14.0 12.7 %collective-permute-start.1 = (f32[8,16,16]{2,1,0:T(8,128)S(1)}, f32[8,16,16]{2,1,0:T(8,128)S(1)}, u32[]{:S(2)}, u32[]{:S(2)}) collective-permute-start(f32[8,16,16]{2,1,0:T(8,128)S(1)} %get-tuple-element.26), channel_id=1, source_target_pairs={{0,1},{1,0},{2,3},{3,2},{4,5},{5,4},{6,7},{7,6},{8,9},{9,8},{10,11... | collective-permute-start | bytes 24584 | tf_op jit(solution)/shard_map/ppermute | solution.py:309
  23.6 0.7 copy-start.8
  24.3 1.0 copy-start.10
  24.3 1.0 copy-start.11
  24.3 1.0 copy-start.12
  24.4 2.3 copy-start.5
  24.5 17.6 %copy-start.1 = (bf16[1664,256]{1,0:T(8,128)(2,1)}, bf16[1664,256]{1,0:T(8,128)(2,1)S(1)}, u32[]{:S(2)}) copy-start(bf16[1664,256]{1,0:T(8,128)(2,1)S(1)} %get-tuple-element.47.s_w2) | copy-start | bytes 2555908
  24.5 17.6 %copy-start.2 = (bf16[1664,256]{1,0:T(8,128)(2,1)}, bf16[1664,256]{1,0:T(8,128)(2,1)S(1)}, u32[]{:S(2)}) copy-start(bf16[1664,256]{1,0:T(8,128)(2,1)S(1)} %get-tuple-element.46.t_w2) | copy-start | bytes 2555908
  26.8 15.2 %collective-permute-start.2 = (f32[8,9,160]{2,1,0:T(8,128)S(1)}, f32[8,9,160]{2,1,0:T(8,128)S(1)}, u32[]{:S(2)}, u32[]{:S(2)}) collective-permute-start(f32[8,9,160]{2,1,0:T(8,128)S(1)} %get-tuple-element.19), channel_id=1, source_target_pairs={{0,2},{2,4},{4,6},{6,8},{8,10},{10,12},{12,14},{14,16},{16,18},{18... | collective-permute-start | bytes 138248 | tf_op jit(solution)/shard_map/ppermute | solution.py:313
  28.3 13.7 %collective-permute-start.3 = (f32[8,9,160]{2,1,0:T(8,128)S(1)}, f32[8,9,160]{2,1,0:T(8,128)S(1)}, u32[]{:S(2)}, u32[]{:S(2)}) collective-permute-start(f32[8,9,160]{2,1,0:T(8,128)S(1)} %get-tuple-element.20), channel_id=1, source_target_pairs={{2,0},{4,2},{6,4},{8,6},{10,8},{12,10},{14,12},{16,14},{18,16},{20... | collective-permute-start | bytes 138248 | tf_op jit(solution)/shard_map/ppermute | solution.py:314
  214.8 5.5 %copy-start.3 = (f32[128,1152]{1,0:T(8,128)S(1)}, f32[128,1152]{1,0:T(8,128)}, u32[]{:S(2)}) copy-start(f32[128,1152]{1,0:T(8,128)} %get-tuple-element.16) | copy-start | bytes 1769476
Sparse Core Ops, SparseCore 0:
  81.7 133.0 all-reduce.21
where the time goes:
time: 230 us; the launch traced here: 229 us
  waiting for transfers between devices  131 us (57%)
  Pallas kernels  37.4 us (16%)
  between operations  25.8 us (11%)
  local copies, waits for them, and re-layouts  13.9 us (6%)
  other arithmetic  13.1 us (6%)
  starting transfers between devices  5.91 us (3%)
  matrix products  2.31 us (1%)
    psum x1, waiting for transfers between devices, local(): g2, g1 = lax.psum((g2, g1), ('lat', 'lon'))  131 us
    pallas_call x1, Pallas kernels, local(): pl.pallas_call(functools.partial(kernel, rows, pairs, center), out_shape=...  37.4 us
  transfers between devices with their start and end apart: 5, of which 1 were waited for; matrix products, arithmetic and copies ran while one was open for 8% of the time, Pallas kernels for 0%

commit v1 on v0

v1 whole, which is shorter than its diff:
```python
import functools

import jax
import jax.numpy as jnp
import numpy as np
from jax import lax
from jax.experimental import pallas as pl
from jax.experimental.pallas import tpu as pltpu
from jax.sharding import PartitionSpec as P

SCHED = 18
HALO = 9
SIDE = 16
C = 128
F32 = jnp.float32
BF16 = jnp.bfloat16


def scalar_table():
    ramp = np.arange(SCHED, dtype=np.float64) / (SCHED - 1)
    top, bottom = 80.0 ** (1.0 / 7.0), 0.02 ** (1.0 / 7.0)
    sigma = (top + ramp * (bottom - top)) ** 7.0
    rows = []
    for n in range(SCHED - 2):
        sig = sigma[n : n + 3]
        s0, s1, s2 = sig
        q2 = sig * sig + 0.25
        q = np.sqrt(q2)
        lam = q2[0] / (s0 * s0 * 0.25)
        h0, h1 = s1 - s0, s2 - s1
        rows.append(
            [*sig, *(1.0 / q), *(sig * sig / q2), *(0.25 / q2), *(sig * 0.5 / q)]
            + [h0, h1, h0 / s0, h0 / s1, h1 / s1, h1 / s2, s0 / (s2 - s0)]
            + [s0 * 0.5 / q[0] * 2.0 * lam]
        )
    return np.asarray(rows, np.float32)


N_SCALARS = 23
MESH = pl.DeviceIdType.MESH


def halo_kernel(lat_n, lon_n, offsets, table, index, clean, noise, mean, out, send, recv):
    y, x = lax.axis_index("lat"), lax.axis_index("lon")
    partners = []
    for dy in (0, 1, -1):
        for n, dx in enumerate(offsets):
            if dy or dx:
                back = [(-dx - other) % lon_n for other in offsets].index(0)
                partners.append(
                    (lax.rem(y + dy + lat_n, lat_n), lax.rem(x + dx + lon_n, lon_n), 1 - dy, back)
                )
    barrier = pltpu.get_barrier_semaphore()
    for py, px, _, _ in partners:
        pl.semaphore_signal(barrier, inc=1, device_id=(py, px), device_id_type=MESH)
    out[1, 0, 0:4] = clean[...] + table[index[0] * N_SCALARS] * noise[...]
    out[1, 0, 4:8] = mean[...]
    pl.semaphore_wait(barrier, len(partners))
    copies = []
    for k, (py, px, sy, sx) in enumerate(partners):
        copy = pltpu.make_async_remote_copy(
            src_ref=out.at[1, 0],
            dst_ref=out.at[sy, sx],
            send_sem=send.at[k],
            recv_sem=recv.at[k],
            device_id=(py, px),
            device_id_type=MESH,
        )
        copy.start()
        copies.append(copy)
    for copy in copies:
        copy.wait()


def sum_kernel(
    inner, depth, lon_n, chunk, piece,
    part, lift, first_ref, second_ref,
    outgoing, plane_in, held, line_in, line_all, plane_all, send, recv,
):
    y, x = lax.axis_index("lat"), lax.axis_index("lon")
    plane = inner * lon_n
    line = lax.div(y, inner)
    spot = lax.rem(y, inner) * lon_n + x

    def in_plane(step):
        other = lax.rem(spot + step, plane)
        return other, (line * inner + lax.div(other, lon_n), lax.rem(other, lon_n))

    def in_line(step):
        other = lax.rem(line + step, depth)
        return other, (other * inner + lax.rem(y, inner), x)

    barrier = pltpu.get_barrier_semaphore()
    for step in range(1, plane):
        pl.semaphore_signal(barrier, inc=1, device_id=in_plane(step)[1], device_id_type=MESH)
    for step in range(1, depth):
        pl.semaphore_signal(barrier, inc=1, device_id=in_line(step)[1], device_id_type=MESH)
    for n in range(plane):
        outgoing[n] = part[n * chunk : (n + 1) * chunk].astype(BF16)
    pl.semaphore_wait(barrier, plane + depth - 2)

    used = [0]

    def exchange(count, where, source, target):
        copies = []
        for step in range(1, count):
            other, device = where(step)
            k = used[0]
            used[0] += 1
            copy = pltpu.make_async_remote_copy(
                src_ref=source(other),
                dst_ref=target(step),
                send_sem=send.at[k],
                recv_sem=recv.at[k],
                device_id=device,
                device_id_type=MESH,
            )
            copy.start()
            copies.append(copy)
        for copy in copies:
            copy.wait()

    exchange(plane, in_plane, lambda o: outgoing.at[o], lambda step: plane_in.at[step - 1])
    own = part[pl.ds(pl.multiple_of(spot * chunk, 8), chunk)]
    for n in range(plane - 1):
        own = own + plane_in[n].astype(F32)
    for n in range(depth):
        held[n] = own[n * piece : (n + 1) * piece]
    exchange(depth, in_line, lambda o: held.at[o], lambda step: line_in.at[step - 1])
    whole = held[line]
    for n in range(depth - 1):
        whole = whole + line_in[n]
    line_all[line] = whole
    exchange(depth, in_line, lambda o: line_all.at[line], lambda step: line_all.at[line])
    plane_all[spot] = line_all[...].reshape(chunk, 128).astype(BF16)
    exchange(plane, in_plane, lambda o: plane_all.at[spot], lambda step: plane_all.at[spot])

    total = plane_all[...].reshape(plane * chunk, 128).astype(F32)
    size = 1.0 / (9 * C * C)
    second = [total[t * C : (t + 1) * C] for t in range(9)]
    spots = total[9 * C : 10 * C]
    tall = jnp.concatenate([lift[...]] * 16, axis=0)
    group = lax.broadcasted_iota(jnp.int32, (128, 128), 0) // 8
    first = [
        jnp.dot(
            spots,
            jnp.where(group == 4 * (t // 3) + t % 3, tall, 0.0),
            precision=lax.Precision.HIGHEST,
            preferred_element_type=F32,
        )
        for t in range(9)
    ]
    for blocks, ref in ((first, first_ref), (second, second_ref)):
        squares = blocks[0] * blocks[0]
        for t in range(1, 9):
            squares = squares + blocks[t] * blocks[t]
        factor = lax.rsqrt(jnp.sum(squares, keepdims=True) * size + 1e-06)
        for t in range(9):
            ref[:, t, :] = blocks[t] * factor


def silu(v):
    u = 0.5 * v
    return u + u * jnp.tanh(u)


def silu_slope(v):
    sig = 0.5 + 0.5 * jnp.tanh(0.5 * v)
    return sig * (1.0 + v * (1.0 - sig))


def kernel(
    rows, pairs, center,
    table, index, blocks_in, taps, lifts, projs,
    tgt_ref, sum_ref,
    x0, xa, xb, fld, u2, x4, dz4, slope1, slope2, dpre,
    t_w1, t_w2, t_pr, s_w1, s_w2, s_pr, s_r, s_pt, joined, turned,
):
    total = rows + 2 * HALO
    me = lax.axis_index("lat")
    top = me == 0
    bottom = me == lax.axis_size("lat") - 1
    base = index[0] * N_SCALARS
    sc = [table[base + k] for k in range(N_SCALARS)]
    lane = lax.broadcasted_iota(jnp.int32, (1, 1, 128), 2)
    lane_a = lane // 32
    lane_j = lane % 32 // 8
    is_x = lane % 8 < 4

    def zero_edges(ref):
        @pl.when(top)
        def _():
            ref[0:HALO] = jnp.zeros((HALO,) + ref.shape[1:], ref.dtype)

        @pl.when(bottom)
        def _():
            ref[HALO + rows : total] = jnp.zeros((HALO,) + ref.shape[1:], ref.dtype)

    def blocks(first, last, size, body):
        count = -(-(last - first) // size)

        def step(i, carry):
            body(jnp.minimum(first + i * size, last - size))
            return carry

        lax.fori_loop(0, count, step, 0)

    cols = 2 * center
    ch_of = lax.broadcasted_iota(jnp.int32, (8, 128), 0)
    lane_of = lax.broadcasted_iota(jnp.int32, (8, 128), 1)
    sel = jnp.where((lane_of % 8 == ch_of) & (lane_of < 96), 1.0, 0.0).astype(F32)
    odd_lane = (lane_j[0] == 0) | (lane_j[0] == 2)
    last_slot = blocks_in.shape[1] - 1

    def load_rows(slot, source, first, count):
        def step(i, carry):
            def turn(part):
                return lax.dot_general(
                    part, sel, (((0,), (0,)), ((), ())),
                    precision=lax.Precision.HIGHEST, preferred_element_type=F32,
                )

            turned[0:cols] = turn(blocks_in[slot, 0, :, source + i, :])
            turned[cols : cols + SIDE] = turn(blocks_in[slot, 1, :, source + i, :])[:SIDE]
            turned[cols + SIDE : cols + 2 * SIDE] = turn(
                blocks_in[slot, last_slot, :, source + i, :]
            )[cols - SIDE :]
            even = turned[pl.ds(0, pairs, stride=2)]
            odd = turned[pl.ds(1, pairs, stride=2)]
            x0[first + i] = jnp.where(odd_lane, odd, even)
            return carry

        lax.fori_loop(0, count, step, 0)

    load_rows(0, rows - HALO, 0, HALO)
    load_rows(1, 0, HALO, rows)
    load_rows(2, 0, HALO + rows, HALO)
    zero_edges(x0)

    def place(ref, t, block):
        a, b = divmod(t, 3)
        for side in range(2):
            at = (4 * a + b + side) * C
            ref[at : at + C, side * C : (side + 1) * C] = block

    for ref in (t_w2, s_w2, s_r):
        ref[...] = jnp.zeros_like(ref)
    none = jnp.zeros((8, C), BF16)
    for net, w1, w2, pr in ((0, t_w1, t_w2, t_pr), (1, s_w1, s_w2, s_pr)):
        joined[...] = jnp.zeros_like(joined)
        for t in range(9):
            a, b = divmod(t, 3)
            mixed = lax.dot_general(
                lifts[net], taps[2 * net, t], (((1,), (1,)), ((), ())),
                preferred_element_type=F32,
            )
            for side in range(2):
                at = a * 32 + (b + side) * 8
                joined[at : at + 8, side * C : (side + 1) * C] = mixed
            place(w2, t, taps[2 * net + 1, t].T)
        high = joined[...].astype(BF16)
        w1[0:128] = high
        w1[128:256] = (joined[...] - high.astype(F32)).astype(BF16)
        w2[12 * C + 40 : 12 * C + 56] = jnp.concatenate(
            [
                jnp.concatenate([lifts[net], none], axis=1),
                jnp.concatenate([none, lifts[net]], axis=1),
            ],
            axis=0,
        )
        flat_lane = lax.broadcasted_iota(jnp.int32, (128, 128), 1)
        flat_row = lax.broadcasted_iota(jnp.int32, (8, 128), 0)
        flat_col = lax.broadcasted_iota(jnp.int32, (8, 128), 1)
        pick = jnp.where((flat_col % 8 == flat_row) & (flat_row < 4), 1.0, 0.0).astype(BF16)
        wide = lax.dot_general(
            projs[net], pick, (((0,), (0,)), ((), ())), preferred_element_type=F32
        )
        slot = flat_lane % 32 // 8
        odd_slot = (slot == 0) | (slot == 2)
        inside = flat_lane < 96
        pr[0:C] = jnp.where(inside & jnp.logical_not(odd_slot), wide, 0.0).astype(BF16)
        pr[C : 2 * C] = jnp.where(inside & odd_slot, wide, 0.0).astype(BF16)
    for t in range(9):
        place(s_r, t, taps[3, 8 - t])
    s_pt[...] = jnp.zeros_like(s_pt)
    s_pt[40:56] = jnp.concatenate(
        [
            jnp.concatenate([projs[1], none], axis=1),
            jnp.concatenate([none, projs[1]], axis=1),
        ],
        axis=0,
    )

    def spread(value, ref, r, nb):
        for n in range(nb):
            row = value[n]
            ref[r + n, :, 0:128] = pltpu.roll(row[:, 128:], 1, 0).astype(BF16)
            ref[r + n, :, 128:384] = row.astype(BF16)
            ref[r + n, :, 384:512] = pltpu.roll(row[:, :128], pairs - 1, 0).astype(BF16)

    def conv1(state, q_inv, w1, first, last, nb, save):
        scale = jnp.where(is_x, q_inv, 1.0)

        def body(r):
            xs = state[pl.ds(r - 1, nb + 2)] * scale
            shifted = []
            for n in range(nb + 2):
                row = xs[n]
                back = pltpu.roll(row, 1, 0)
                ahead = pltpu.roll(row, pairs - 1, 0)
                shifted.append(jnp.where(lane_j[0] == 0, back, jnp.where(lane_j[0] == 3, ahead, row)))
            u = jnp.stack(
                [
                    jnp.where(
                        lane_a[0] == 0,
                        shifted[n],
                        jnp.where(lane_a[0] == 1, shifted[n + 1], shifted[n + 2]),
                    )
                    for n in range(nb)
                ]
            ).astype(BF16)
            u2[pl.ds(r, nb)] = u
            flat = u.reshape(nb * pairs, 128)
            pre = jnp.dot(
                jnp.concatenate([flat, flat], axis=1), w1[...], preferred_element_type=F32
            ).reshape(nb, pairs, 256)
            spread(silu(pre), x4, r, nb)
            if save:
                slope1[pl.ds(r, nb)] = silu_slope(pre)

        blocks(first, last, nb, body)
        zero_edges(x4)

    def conv2(w2, pr, first, last, nb, save):
        def body(r):
            lhs = jnp.concatenate(
                [x4[pl.ds(r + a - 1, nb)].reshape(nb * pairs, 512) for a in range(3)]
                + [u2[pl.ds(r, nb)].reshape(nb * pairs, 128)],
                axis=1,
            )
            z = jnp.dot(lhs, w2[...], preferred_element_type=F32)
            g = silu(z).astype(BF16)
            fld[pl.ds(r, nb)] = jnp.dot(g, pr[...], preferred_element_type=F32).reshape(
                nb, pairs, 128
            )
            if save:
                slope2[pl.ds(r, nb)] = silu_slope(z).reshape(nb, pairs, 256)

        blocks(first, last, nb, body)
        zero_edges(fld)

    s0, s1, s2 = sc[0], sc[1], sc[2]
    q_inv = [sc[3], sc[4], sc[5]]
    rest = [sc[6], sc[7], sc[8]]
    keep = [sc[9], sc[10], sc[11]]
    gain = [sc[12], sc[13], sc[14]]
    h0, h1 = sc[15], sc[16]
    h0_a, h0_b, h1_b, h1_c = sc[17], sc[18], sc[19], sc[20]
    back = sc[21]
    pull = sc[22]

    def teacher(state, level, first):
        last = total - first
        conv1(state, q_inv[level], t_w1, first, last, 4, False)
        conv2(t_w2, t_pr, first + 1, last - 1, 6, False)

    def update(dst, first, fn):
        def body(r):
            at = pl.ds(r, 2)
            dst[at] = fn(at)

        blocks(first, total - first, 2, body)

    def euler(src, dst, first, level, ratio):
        cx = jnp.where(is_x, 1.0 + ratio * rest[level], 1.0)
        cf = ratio * gain[level]
        update(dst, first, lambda at: src[at] * cx - fld[at] * cf)

    def correct(src, guess, dst, first, level, ratio):
        cx = jnp.where(is_x, 0.5 + 0.5 * ratio * rest[level], 0.5)
        cf = 0.5 * ratio * gain[level]
        update(dst, first, lambda at: 0.5 * src[at] + guess[at] * cx - fld[at] * cf)

    teacher(x0, 0, 1)
    euler(x0, xa, 2, 0, h0_a)
    teacher(xa, 1, 3)
    correct(x0, xa, xb, 4, 1, h0_b)
    teacher(xb, 1, 5)
    euler(xb, xa, 6, 1, h1_b)
    teacher(xa, 2, 7)
    correct(xb, xa, xb, 8, 2, h1_c)

    def make_target(at):
        start = x0[at]
        return start - (xb[at] - start) * back

    update(xa, 8, make_target)

    def emit(i, carry):
        row = xa[HALO + i]
        turned[pl.ds(0, pairs, stride=2)] = row
        turned[pl.ds(1, pairs, stride=2)] = pltpu.roll(row, 120, 1)
        flat = turned[0:cols].T
        tgt_ref[:, i, :] = flat[8:12]
        return carry

    lax.fori_loop(0, rows, emit, 0)

    conv1(x0, q_inv[0], s_w1, 7, total - 7, 4, True)
    conv2(s_w2, s_pr, 8, total - 8, 6, True)

    def backward(r):
        at = pl.ds(r, 2)
        d_field = jnp.where(
            is_x, pull * (keep[0] * x0[at] + gain[0] * fld[at] - xa[at]), 0.0
        ).astype(BF16)
        d_gated = jnp.dot(
            d_field.reshape(2 * pairs, 128), s_pt[...], preferred_element_type=F32
        ).reshape(2, pairs, 256)
        spread(d_gated * slope2[at], dz4, r, 2)

    blocks(8, total - 8, 2, backward)
    zero_edges(dz4)

    cells = rows * center
    dims = (((0,), (0,)), ((), ()))
    middle = pl.ds(HALO, rows)
    dz = dz4[middle, 0:center, 128:384].reshape(cells, 256)
    for a in range(3):
        near = x4[pl.ds(HALO - 1 + a, rows), 0:center, :].reshape(cells, 512)
        grad = lax.dot_general(dz, near, dims, preferred_element_type=F32)
        for b in range(3):
            sum_ref[3 * a + b] = (
                grad[:128, b * C : (b + 1) * C] + grad[128:, (b + 1) * C : (b + 2) * C]
            )

    def conv3(r):
        lhs = jnp.concatenate(
            [dz4[pl.ds(r + a - 1, 4)].reshape(4 * pairs, 512) for a in range(3)], axis=1
        )
        dh = jnp.dot(lhs, s_r[...], preferred_element_type=F32).reshape(4, pairs, 256)
        dpre[pl.ds(r - HALO, 4)] = (dh * slope1[pl.ds(r, 4)]).astype(BF16)

    blocks(HALO, HALO + rows, 4, conv3)
    d_before = dpre[:, 0:center, :].reshape(cells, 256)
    near = u2[middle, 0:center, :].reshape(cells, 128)
    grad = lax.dot_general(d_before, near, dims, preferred_element_type=F32)
    sum_ref[9] = grad[:128] + pltpu.roll(grad[128:], 120, 1)


def local(
    clean, noise, mean_field, sigma_index,
    teacher_lift, teacher_first, teacher_second, teacher_proj,
    student_lift, student_first, student_second, student_proj,
):
    rows, cols = clean.shape[1:]
    lat_n, lon_n = lax.axis_size("lat"), lax.axis_size("lon")
    total, pairs, center = rows + 2 * HALO, (cols + 2 * SIDE) // 2, cols // 2
    vmem = pl.BlockSpec(memory_space=pltpu.VMEM)
    smem = pl.BlockSpec(memory_space=pltpu.SMEM)
    table = jnp.asarray(scalar_table().reshape(-1))

    offsets = [0, 1] if lon_n == 2 else [0, 1, -1]
    slots = len(offsets)
    links = 3 * slots - 1
    blocks = pl.pallas_call(
        functools.partial(halo_kernel, lat_n, lon_n, offsets),
        out_shape=jax.ShapeDtypeStruct((3, slots, 8, rows, cols), F32),
        in_specs=[smem, smem, vmem, vmem, vmem],
        out_specs=vmem,
        scratch_shapes=[pltpu.SemaphoreType.DMA((links,)), pltpu.SemaphoreType.DMA((links,))],
        compiler_params=pltpu.CompilerParams(
            collective_id=0, has_side_effects=True, vmem_limit_bytes=16 * 1024 * 1024
        ),
    )(table, sigma_index, clean, noise, mean_field)

    taps = jnp.stack(
        [teacher_first, teacher_second, student_first, student_second]
    ).transpose(0, 2, 1, 3)
    lifts = jnp.stack([teacher_lift, student_lift]).transpose(0, 2, 1)
    projs = jnp.pad(jnp.stack([teacher_proj, student_proj]), ((0, 0), (0, 4), (0, 0)))
    target, sums = pl.pallas_call(
        functools.partial(kernel, rows, pairs, center),
        out_shape=[
            jax.ShapeDtypeStruct((4, rows, cols), F32),
            jax.ShapeDtypeStruct((10, C, C), F32),
        ],
        in_specs=[smem, smem] + [vmem] * 4,
        out_specs=[vmem] * 2,
        scratch_shapes=[pltpu.VMEM((total, pairs, 128), F32)] * 4
        + [
            pltpu.VMEM((total, pairs, 128), BF16),
            pltpu.VMEM((total, pairs, 512), BF16),
            pltpu.VMEM((total, pairs, 512), BF16),
            pltpu.VMEM((total, pairs, 256), F32),
            pltpu.VMEM((total, pairs, 256), F32),
            pltpu.VMEM((rows, pairs, 256), BF16),
        ]
        + [
            pltpu.VMEM((2 * C, 2 * C), BF16),
            pltpu.VMEM((13 * C, 2 * C), BF16),
            pltpu.VMEM((2 * C, C), BF16),
        ]
        * 2
        + [
            pltpu.VMEM((12 * C, 2 * C), BF16),
            pltpu.VMEM((C, 2 * C), BF16),
            pltpu.VMEM((C, 2 * C), F32),
            pltpu.VMEM((2 * pairs, 128), F32),
        ],
        compiler_params=pltpu.CompilerParams(vmem_limit_bytes=56 * 1024 * 1024),
    )(table, sigma_index, blocks, taps, lifts, projs)

    inner = 4 if lat_n % 4 == 0 else 1
    depth, plane = lat_n // inner, inner * lon_n
    piece = -(-10 * C // (plane * depth * 8)) * 8
    while piece * depth % 16:
        piece += 8
    chunk = piece * depth
    part = sums.reshape(10 * C, C)
    if plane * chunk > 10 * C:
        part = jnp.pad(part, ((0, plane * chunk - 10 * C), (0, 0)))
    links = 2 * (plane + depth - 2)
    update_first, update_second = pl.pallas_call(
        functools.partial(sum_kernel, inner, depth, lon_n, chunk, piece),
        out_shape=[jax.ShapeDtypeStruct((C, 9, C), F32)] * 2,
        in_specs=[vmem] * 2,
        out_specs=[vmem] * 2,
        scratch_shapes=[
            pltpu.VMEM((plane, chunk, 128), BF16),
            pltpu.VMEM((plane - 1, chunk, 128), BF16),
            pltpu.VMEM((depth, piece, 128), F32),
            pltpu.VMEM((depth - 1, piece, 128), F32),
            pltpu.VMEM((depth, piece, 128), F32),
            pltpu.VMEM((plane, chunk, 128), BF16),
            pltpu.SemaphoreType.DMA((links,)),
            pltpu.SemaphoreType.DMA((links,)),
        ],
        compiler_params=pltpu.CompilerParams(
            collective_id=1, has_side_effects=True, vmem_limit_bytes=32 * 1024 * 1024
        ),
    )(part, student_lift.T.astype(F32))
    return (target, update_first, update_second)


def solution(mesh):
    grid = P(None, "lat", "lon")
    return jax.shard_map(
        local,
        mesh=mesh,
        in_specs=(grid, grid, grid) + (P(),) * 9,
        out_specs=(grid, P(), P()),
        check_vma=False,
    )
```

time: 230 us -> 95.4 us (0.41)
  waiting for transfers between devices: 131 us -> 0 us
  Pallas kernels: 37.4 us -> 81.1 us
  between operations: 25.8 us -> 1.31 us
  other arithmetic: 13.1 us -> 5.66 us
  local copies, waits for them, and re-layouts: 13.9 us -> 6.77 us
  starting transfers between devices: 5.91 us -> 0 us
  matrix products: 2.31 us -> 0 us
    psum x1 -> x0, waiting for transfers between devices: 131 us -> none  [local(): g2, g1 = lax.psum((g2, g1), ('lat', 'lon'))]
    pallas_call x0 -> x2, Pallas kernels: none -> 32.2 us  [the longest x1 21.6 us: local(): pl.pallas_call(functools.partial(sum_kernel, inner, depth, lon_n, chunk,...]
    pallas_call x1, Pallas kernels: 37.4 us -> 48.8 us  [local(): pl.pallas_call(functools.partial(kernel, rows, pairs, center), out_shape=...]
    ppermute x4 -> x0, starting transfers between devices: 5.87 us -> none  [the longest x1 3.03 us: local(): right = lax.ppermute(cells[:, :, :SIDE], 'lon', [(b, a) for a, b in ring])]
    concatenate x11 -> x0, other arithmetic: 4.34 us -> none  [the longest x5 1.16 us: pair_weights(): both = jnp.concatenate([even, odd], axis=3)]
    unnamed x36 -> x14, local copies, waits for them, and re-layouts: 2.49 us -> 6.77 us
    transpose x0 -> x2, other arithmetic: none -> 3.69 us  [the longest x1 2.39 us: local(): taps = jnp.stack([teacher_first, teacher_second, student_first, student_s...]
    concatenate x4 -> x0, local copies, waits for them, and re-layouts: 3.52 us -> none  [the longest x1 2.52 us: local(): jnp.concatenate([sig, 1.0 / q, sig * sig / q2, 0.25 / q2, sig * 0.5 / q,...]
  transfers between devices with their start and end apart: 5 -> 0, of which waited for: 1 -> 0; matrix products, arithmetic and copies ran while one was open for 8% -> 0% of each run, Pallas kernels for 0% -> 0%
where the time goes in v1:
time: 95.4 us; the launch traced here: 94.8 us
  Pallas kernels  81.1 us (85%)
  local copies, waits for them, and re-layouts  6.77 us (7%)
  other arithmetic  5.66 us (6%)
  between operations  1.31 us (1%)
    pallas_call x1, Pallas kernels, local(): pl.pallas_call(functools.partial(kernel, rows, pairs, center), out_shape=...  48.8 us
    pallas_call x1, Pallas kernels, local(): pl.pallas_call(functools.partial(sum_kernel, inner, depth, lon_n, chunk,...  21.6 us
    pallas_call x1, Pallas kernels, local(): pl.pallas_call(functools.partial(halo_kernel, lat_n, lon_n, offsets), out...  10.6 us
    unnamed x14, local copies, waits for them, and re-layouts  6.77 us
    transpose x1, other arithmetic, local(): taps = jnp.stack([teacher_first, teacher_second, student_first, student_s...  2.39 us

profile of v1, /device:TPU:0, one launch (start us, length us, event | category | flops | bytes accessed | tf_op | source)
XLA Modules:
  0.0 94.8 jit_solution(7470556643939930629)
XLA Ops:
  1.3 1.3 %maximum_bitcast_fusion.1.lifts = bf16[2,8,128]{2,1,0:T(8,128)(2,1)} fusion(bf16[1,128,8]{1,2,0:T(8,128)(2,1)} %bitcast.20, bf16[1,128,8]{1,2,0:T(8,128)(2,1)} %bitcast.21), kind=kLoop, calls=%fused_computation.5 | loop fusion | flops 2048 | bytes 8192 | tf_op jit(solution)/shard_map/transpose | solution.py:480
  2.6 1.3 %fusion.2.projs = bf16[2,8,128]{2,1,0:T(8,128)(2,1)} fusion(bf16[1,4,128]{2,1,0:T(4,128)(2,1)} %bitcast.22, bf16[1,4,128]{2,1,0:T(4,128)(2,1)} %bitcast.23), kind=kLoop, calls=%fused_computation.4 | loop fusion | flops 14336 | bytes 6144 | tf_op jit(solution)/shard_map/stack | solution.py:481
  3.9 0.7 convert_bitcast_fusion.lift
  4.5 0.0 copy-start.2
  4.6 0.8 copy-done.2
  5.3 0.0 copy-start.3
  5.3 0.8 copy-done.3
  6.1 0.0 copy-start.4
  6.1 0.8 copy-done.4
  6.8 0.0 copy-start.5
  6.8 0.7 copy-done.5
  7.5 10.6 %shard_map.148.blocks_in = f32[3,2,8,16,128]{4,3,2,1,0:T(8,128)S(1)} custom-call(f32[368]{0:T(512)S(1)} %copy-done.5, s32[1]{0:T(128)S(6)} %copy.18.index, f32[4,16,128]{2,1,0:T(8,128)S(1)} %copy-done.2, f32[4,16,128]{2,1,0:T(8,128)S(1)} %copy-done.3, f32[4,16,128]{2,1,0:T(8,128)S(1)} %copy-done.4), custom_call_target="tpu_custom_call" | custom-call | tf_op jit(solution)/shard_map/pallas_call | solution.py:466
  18.1 0.0 copy-start
  18.1 0.7 copy-done
  18.9 2.4 %maximum_bitcast_fusion.taps = bf16[4,9,128,128]{3,2,1,0:T(8,128)(2,1)} fusion(bf16[1,128,9,128]{3,1,2,0:T(8,128)(2,1)} %bitcast.16, bf16[1,128,9,128]{3,1,2,0:T(8,128)(2,1)} %bitcast.17, bf16[1,128,9,128]{3,1,2,0:T(8,128)(2,1)} %bitcast.18, bf16[1,128,9,128]{3,1,2,0:T(8,128)(2,1)} %bitcast.19), kind=kLoop, calls=%fused_computation | loop fusion | flops 1769472 | bytes 2359296 | tf_op jit(solution)/shard_map/transpose | solution.py:479
  21.3 48.8 %shard_map.149 = (f32[4,16,128]{2,1,0:T(8,128)}, f32[10,128,128]{2,1,0:T(8,128)}) custom-call(f32[368]{0:T(512)} %constant.5.clone.table, s32[1]{0:T(128)S(6)} %copy.18.index, f32[3,2,8,16,128]{4,3,2,1,0:T(8,128)} %copy-done, bf16[4,9,128,128]{3,2,1,0:T(8,128)(2,1)} %maximum_bitcast_fusion.taps, bf16[2,8,128]{2,1,0:T(8,128)(2,1)} %maximum_bitcast_fusion.1.lifts, ...), custom_call_target="tpu_custom_call" | custom-call | tf_op jit(solution)/shard_map/pallas_call | solution.py:482
  70.1 0.0 copy-start.1
  70.1 1.1 %copy-done.1 = f32[10,128,128]{2,1,0:T(8,128)S(1)} copy-done((f32[10,128,128]{2,1,0:T(8,128)S(1)}, f32[10,128,128]{2,1,0:T(8,128)}, u32[]{:S(2)}) %copy-start.1) | copy-done | bytes 655384
  71.2 21.6 %shard_map.150 = (f32[128,9,128]{2,1,0:T(8,128)S(1)}, f32[128,9,128]{2,1,0:T(8,128)S(1)}) custom-call(f32[1280,128]{1,0:T(8,128)S(1)} %bitcast.15, f32[8,128]{1,0:T(8,128)S(1)} %convert_bitcast_fusion.lift), custom_call_target="tpu_custom_call" | custom-call | tf_op jit(solution)/shard_map/pallas_call | solution.py:524
  92.8 1.0 %copy.16 = f32[128,9,128]{2,0,1:T(8,128)} copy(f32[128,9,128]{2,1,0:T(8,128)S(1)} %get-tuple-element.12) | data formatting | bytes 1179648
  93.8 1.0 %copy.17 = f32[128,9,128]{2,0,1:T(8,128)} copy(f32[128,9,128]{2,1,0:T(8,128)S(1)} %get-tuple-element.13) | data formatting | bytes 1179648
Async XLA Ops:
  4.5 0.8 copy-start.2
  5.3 0.8 copy-start.3
  6.1 0.8 copy-start.4
  6.8 0.7 copy-start.5
  18.1 0.7 copy-start
  70.1 1.1 %copy-start.1 = (f32[10,128,128]{2,1,0:T(8,128)S(1)}, f32[10,128,128]{2,1,0:T(8,128)}, u32[]{:S(2)}) copy-start(f32[10,128,128]{2,1,0:T(8,128)} %get-tuple-element.8) | copy-start | bytes 1966084

commit v2 on v1

--- a/solution.py
+++ b/solution.py
@@ -139,7 +139,7 @@
     size = 1.0 / (9 * C * C)
     second = [total[t * C : (t + 1) * C] for t in range(9)]
     spots = total[9 * C : 10 * C]
-    tall = jnp.concatenate([lift[...]] * 16, axis=0)
+    tall = jnp.concatenate([lift[...].astype(F32).T] * 16, axis=0)
     group = lax.broadcasted_iota(jnp.int32, (128, 128), 0) // 8
     first = [
         jnp.dot(
@@ -171,7 +171,7 @@
 
 def kernel(
     rows, pairs, center,
-    table, index, blocks_in, taps, lifts, projs,
+    table, index, blocks_in, taps, t_lift, s_lift, t_proj, s_proj,
     tgt_ref, sum_ref,
     x0, xa, xb, fld, u2, x4, dz4, slope1, slope2, dpre,
     t_w1, t_w2, t_pr, s_w1, s_w2, s_pr, s_r, s_pt, joined, turned,
@@ -198,33 +198,31 @@
 
     def blocks(first, last, size, body):
         count = -(-(last - first) // size)
+        room, gaps = last - first - size, max(count - 1, 1)
 
         def step(i, carry):
-            body(jnp.minimum(first + i * size, last - size))
+            body(first + i * room // gaps)
             return carry
 
         lax.fori_loop(0, count, step, 0)
 
     cols = 2 * center
-    ch_of = lax.broadcasted_iota(jnp.int32, (8, 128), 0)
-    lane_of = lax.broadcasted_iota(jnp.int32, (8, 128), 1)
-    sel = jnp.where((lane_of % 8 == ch_of) & (lane_of < 96), 1.0, 0.0).astype(F32)
     odd_lane = (lane_j[0] == 0) | (lane_j[0] == 2)
     last_slot = blocks_in.shape[1] - 1
+    column = lax.broadcasted_iota(jnp.int32, (8, cols), 1)
 
     def load_rows(slot, source, first, count):
         def step(i, carry):
-            def turn(part):
-                return lax.dot_general(
-                    part, sel, (((0,), (0,)), ((), ())),
-                    precision=lax.Precision.HIGHEST, preferred_element_type=F32,
-                )
-
-            turned[0:cols] = turn(blocks_in[slot, 0, :, source + i, :])
-            turned[cols : cols + SIDE] = turn(blocks_in[slot, 1, :, source + i, :])[:SIDE]
-            turned[cols + SIDE : cols + 2 * SIDE] = turn(
-                blocks_in[slot, last_slot, :, source + i, :]
-            )[cols - SIDE :]
+            own = blocks_in[slot, 0, :, source + i, :]
+            beside = jnp.where(
+                column < SIDE,
+                blocks_in[slot, 1, :, source + i, :],
+                blocks_in[slot, last_slot, :, source + i, :],
+            )
+            turned[0:cols] = jnp.concatenate([own] * 16, axis=0).T
+            sides = jnp.concatenate([beside] * 16, axis=0).T
+            turned[cols : cols + SIDE] = sides[:SIDE]
+            turned[cols + SIDE : cols + 2 * SIDE] = sides[cols - SIDE :]
             even = turned[pl.ds(0, pairs, stride=2)]
             odd = turned[pl.ds(1, pairs, stride=2)]
             x0[first + i] = jnp.where(odd_lane, odd, even)
@@ -246,6 +244,12 @@
     for ref in (t_w2, s_w2, s_r):
         ref[...] = jnp.zeros_like(ref)
     none = jnp.zeros((8, C), BF16)
+    four = jnp.zeros((4, C), F32)
+    lifts = [ref[...].astype(F32).T.astype(BF16) for ref in (t_lift, s_lift)]
+    projs = [
+        jnp.concatenate([ref[...].astype(F32), four], axis=0).astype(BF16)
+        for ref in (t_proj, s_proj)
+    ]
     for net, w1, w2, pr in ((0, t_w1, t_w2, t_pr), (1, s_w1, s_w2, s_pr)):
         joined[...] = jnp.zeros_like(joined)
         for t in range(9):
@@ -361,7 +365,7 @@
 
     def teacher(state, level, first):
         last = total - first
-        conv1(state, q_inv[level], t_w1, first, last, 4, False)
+        conv1(state, q_inv[level], t_w1, first, last, 8, False)
         conv2(t_w2, t_pr, first + 1, last - 1, 6, False)
 
     def update(dst, first, fn):
@@ -396,15 +400,20 @@
 
     update(xa, 8, make_target)
 
-    def emit(i, carry):
-        row = xa[HALO + i]
-        turned[pl.ds(0, pairs, stride=2)] = row
-        turned[pl.ds(1, pairs, stride=2)] = pltpu.roll(row, 120, 1)
+    for first in range(0, rows, 16):
+        count = min(16, rows - first)
+        even = jnp.zeros((center, 128), F32)
+        odd = even
+        group = lax.broadcasted_iota(jnp.int32, (center, 128), 1) // 8
+        for i in range(count):
+            row = xa[HALO + first + i, 0:center]
+            even = jnp.where(group == i, pltpu.roll(row, (8 * i + 120) % 128, 1), even)
+            odd = jnp.where(group == i, pltpu.roll(row, (8 * i + 112) % 128, 1), odd)
+        turned[pl.ds(0, center, stride=2)] = even
+        turned[pl.ds(1, center, stride=2)] = odd
         flat = turned[0:cols].T
-        tgt_ref[:, i, :] = flat[8:12]
-        return carry
-
-    lax.fori_loop(0, rows, emit, 0)
+        for i in range(count):
+            tgt_ref[:, first + i, :] = flat[8 * i : 8 * i + 4]
 
     conv1(x0, q_inv[0], s_w1, 7, total - 7, 4, True)
     conv2(s_w2, s_pr, 8, total - 8, 6, True)
@@ -477,15 +486,13 @@
     taps = jnp.stack(
         [teacher_first, teacher_second, student_first, student_second]
     ).transpose(0, 2, 1, 3)
-    lifts = jnp.stack([teacher_lift, student_lift]).transpose(0, 2, 1)
-    projs = jnp.pad(jnp.stack([teacher_proj, student_proj]), ((0, 0), (0, 4), (0, 0)))
     target, sums = pl.pallas_call(
         functools.partial(kernel, rows, pairs, center),
         out_shape=[
             jax.ShapeDtypeStruct((4, rows, cols), F32),
             jax.ShapeDtypeStruct((10, C, C), F32),
         ],
-        in_specs=[smem, smem] + [vmem] * 4,
+        in_specs=[smem, smem] + [vmem] * 6,
         out_specs=[vmem] * 2,
         scratch_shapes=[pltpu.VMEM((total, pairs, 128), F32)] * 4
         + [
@@ -509,7 +516,10 @@
             pltpu.VMEM((2 * pairs, 128), F32),
         ],
         compiler_params=pltpu.CompilerParams(vmem_limit_bytes=56 * 1024 * 1024),
-    )(table, sigma_index, blocks, taps, lifts, projs)
+    )(
+        table, sigma_index, blocks, taps,
+        teacher_lift, student_lift, teacher_proj, student_proj,
+    )
 
     inner = 4 if lat_n % 4 == 0 else 1
     depth, plane = lat_n // inner, inner * lon_n
@@ -539,7 +549,7 @@
         compiler_params=pltpu.CompilerParams(
             collective_id=1, has_side_effects=True, vmem_limit_bytes=32 * 1024 * 1024
         ),
-    )(part, student_lift.T.astype(F32))
+    )(part, student_lift)
     return (target, update_first, update_second)
 
 

time: 95.4 us -> 83.4 us (0.87)
  Pallas kernels: 81.1 us -> 69.6 us
  other arithmetic: 5.66 us -> 2.41 us
  local copies, waits for them, and re-layouts: 6.77 us -> 9.58 us
    pallas_call x1, Pallas kernels: 48.8 us -> 37.3 us  [local(): pl.pallas_call(functools.partial(kernel, rows, pairs, center), out_shape=...]
    unnamed x14 -> x18, local copies, waits for them, and re-layouts: 6.77 us -> 9.58 us
    transpose x1 -> x0, other arithmetic: 1.3 us -> none  [local(): lifts = jnp.stack([teacher_lift, student_lift]).transpose(0, 2, 1)]
    another operation x1 -> x0, other arithmetic: 1.29 us -> none  [local(): jnp.stack([teacher_proj, student_proj])]
where the time goes in v2:
time: 83.4 us; the launch traced here: 82.9 us
  Pallas kernels  69.6 us (83%)
  local copies, waits for them, and re-layouts  9.58 us (11%)
  other arithmetic  2.41 us (3%)
  between operations  1.31 us (2%)
    pallas_call x1, Pallas kernels, local(): pl.pallas_call(functools.partial(kernel, rows, pairs, center), out_shape=...  37.3 us
    pallas_call x1, Pallas kernels, local(): pl.pallas_call(functools.partial(sum_kernel, inner, depth, lon_n, chunk,...  21.7 us
    pallas_call x1, Pallas kernels, local(): pl.pallas_call(functools.partial(halo_kernel, lat_n, lon_n, offsets), out...  10.6 us
    unnamed x18, local copies, waits for them, and re-layouts  9.58 us
    transpose x1, other arithmetic, local(): taps = jnp.stack([teacher_first, teacher_second, student_first, student_s...  2.41 us

profile of v2, /device:TPU:0, one launch (start us, length us, event | category | flops | bytes accessed | tf_op | source)
XLA Modules:
  0.0 82.9 jit_solution(16864816548055441873)
XLA Ops:
  1.3 1.4 %copy.17.s_lift.lift = bf16[128,8]{1,0:T(8,128)(2,1)} copy(bf16[128,8]{0,1:T(8,128)(2,1)} %param.21) | data formatting | bytes 4096 | tf_op args[8]
  2.7 1.4 %copy.16.t_lift = bf16[128,8]{1,0:T(8,128)(2,1)} copy(bf16[128,8]{0,1:T(8,128)(2,1)} %param.17) | data formatting | bytes 4096 | tf_op args[4]
  4.1 0.0 copy-start.3
  4.1 0.8 copy-done.3
  4.8 0.0 copy-start.4
  4.8 0.8 copy-done.4
  5.6 0.0 copy-start.5
  5.6 0.8 copy-done.5
  6.4 0.0 copy-start.6
  6.4 0.7 copy-done.6
  7.0 10.6 %shard_map.148.blocks_in = f32[3,2,8,16,128]{4,3,2,1,0:T(8,128)S(1)} custom-call(f32[368]{0:T(512)S(1)} %copy-done.6, s32[1]{0:T(128)S(6)} %copy.21.index, f32[4,16,128]{2,1,0:T(8,128)S(1)} %copy-done.3, f32[4,16,128]{2,1,0:T(8,128)S(1)} %copy-done.4, f32[4,16,128]{2,1,0:T(8,128)S(1)} %copy-done.5), custom_call_target="tpu_custom_call" | custom-call | tf_op jit(solution)/shard_map/pallas_call | solution.py:475
  17.7 0.0 copy-start
  17.7 0.7 copy-done
  18.4 2.4 %maximum_bitcast_fusion.taps = bf16[4,9,128,128]{3,2,1,0:T(8,128)(2,1)} fusion(bf16[1,128,9,128]{3,1,2,0:T(8,128)(2,1)} %bitcast.8, bf16[1,128,9,128]{3,1,2,0:T(8,128)(2,1)} %bitcast.9, bf16[1,128,9,128]{3,1,2,0:T(8,128)(2,1)} %bitcast.10, bf16[1,128,9,128]{3,1,2,0:T(8,128)(2,1)} %bitcast.11), kind=kLoop, calls=%fused_computation | loop fusion | flops 1769472 | bytes 2359296 | tf_op jit(solution)/shard_map/transpose | solution.py:488
  20.8 0.0 copy-start.2
  20.8 37.3 %shard_map.149 = (f32[4,16,128]{2,1,0:T(8,128)}, f32[10,128,128]{2,1,0:T(8,128)}) custom-call(f32[368]{0:T(512)} %constant.2.clone.table, s32[1]{0:T(128)S(6)} %copy.21.index, f32[3,2,8,16,128]{4,3,2,1,0:T(8,128)} %copy-done, bf16[4,9,128,128]{3,2,1,0:T(8,128)(2,1)} %maximum_bitcast_fusion.taps, bf16[128,8]{1,0:T(8,128)(2,1)} %copy.16.t_lift, ...), custom_call_target="tpu_custom_call" | custom-call | tf_op jit(solution)/shard_map/pallas_call | solution.py:489
  58.1 0.0 copy-done.2
  58.1 0.0 copy-start.1
  58.1 1.1 %copy-done.1 = f32[10,128,128]{2,1,0:T(8,128)S(1)} copy-done((f32[10,128,128]{2,1,0:T(8,128)S(1)}, f32[10,128,128]{2,1,0:T(8,128)}, u32[]{:S(2)}) %copy-start.1) | copy-done | bytes 655384
  59.2 21.7 %shard_map.150 = (f32[128,9,128]{2,1,0:T(8,128)S(1)}, f32[128,9,128]{2,1,0:T(8,128)S(1)}) custom-call(f32[1280,128]{1,0:T(8,128)S(1)} %bitcast.7, bf16[128,8]{1,0:T(8,128)(2,1)S(1)} %copy-done.2), custom_call_target="tpu_custom_call" | custom-call | tf_op jit(solution)/shard_map/pallas_call | solution.py:534
  80.9 1.0 %copy.19 = f32[128,9,128]{2,0,1:T(8,128)} copy(f32[128,9,128]{2,1,0:T(8,128)S(1)} %get-tuple-element.12) | data formatting | bytes 1179648
  81.9 1.0 %copy.20 = f32[128,9,128]{2,0,1:T(8,128)} copy(f32[128,9,128]{2,1,0:T(8,128)S(1)} %get-tuple-element.13) | data formatting | bytes 1179648
Async XLA Ops:
  4.1 0.8 copy-start.3
  4.8 0.8 copy-start.4
  5.6 0.8 copy-start.5
  6.4 0.7 copy-start.6
  17.7 0.7 copy-start
  20.8 37.3 %copy-start.2 = (bf16[128,8]{1,0:T(8,128)(2,1)S(1)}, bf16[128,8]{1,0:T(8,128)(2,1)}, u32[]{:S(2)}) copy-start(bf16[128,8]{1,0:T(8,128)(2,1)} %copy.17.s_lift.lift) | copy-start | bytes 6148
  58.1 1.1 %copy-start.1 = (f32[10,128,128]{2,1,0:T(8,128)S(1)}, f32[10,128,128]{2,1,0:T(8,128)}, u32[]{:S(2)}) copy-start(f32[10,128,128]{2,1,0:T(8,128)} %get-tuple-element.8) | copy-start | bytes 1966084

commit v3 on v2

--- a/solution.py
+++ b/solution.py
@@ -40,47 +40,42 @@
 MESH = pl.DeviceIdType.MESH
 
 
-def halo_kernel(lat_n, lon_n, offsets, table, index, clean, noise, mean, out, send, recv):
+def silu(v):
+    u = 0.5 * v
+    return u + u * jnp.tanh(u)
+
+
+def silu_slope(v):
+    sig = 0.5 + 0.5 * jnp.tanh(0.5 * v)
+    return sig * (1.0 + v * (1.0 - sig))
+
+
+def kernel(
+    rows, pairs, center, lat_n, lon_n, offsets, inner, chunk_a, chunk_b,
+    table, index, clean, noise, mean, t_first, t_second, s_first, s_second,
+    t_lift, s_lift, t_proj, s_proj,
+    tgt_ref, first_ref, second_ref,
+    x0, xa, xb, fld, u2, x4, dz4, slope1, slope2, dpre,
+    t_w1, t_w2, t_pr, s_w1, s_w2, s_pr, s_r, s_pt, joined, turned,
+    blocks_in, sum_a, sum_b, out_a, out_b, in_a, in_b, held, line_in, line_all, plane_all,
+    send, recv,
+):
+    total = rows + 2 * HALO
     y, x = lax.axis_index("lat"), lax.axis_index("lon")
-    partners = []
-    for dy in (0, 1, -1):
-        for n, dx in enumerate(offsets):
-            if dy or dx:
-                back = [(-dx - other) % lon_n for other in offsets].index(0)
-                partners.append(
-                    (lax.rem(y + dy + lat_n, lat_n), lax.rem(x + dx + lon_n, lon_n), 1 - dy, back)
-                )
-    barrier = pltpu.get_barrier_semaphore()
-    for py, px, _, _ in partners:
-        pl.semaphore_signal(barrier, inc=1, device_id=(py, px), device_id_type=MESH)
-    out[1, 0, 0:4] = clean[...] + table[index[0] * N_SCALARS] * noise[...]
-    out[1, 0, 4:8] = mean[...]
-    pl.semaphore_wait(barrier, len(partners))
-    copies = []
-    for k, (py, px, sy, sx) in enumerate(partners):
-        copy = pltpu.make_async_remote_copy(
-            src_ref=out.at[1, 0],
-            dst_ref=out.at[sy, sx],
-            send_sem=send.at[k],
-            recv_sem=recv.at[k],
-            device_id=(py, px),
-            device_id_type=MESH,
-        )
-        copy.start()
-        copies.append(copy)
-    for copy in copies:
-        copy.wait()
-
-
-def sum_kernel(
-    inner, depth, lon_n, chunk, piece,
-    part, lift, first_ref, second_ref,
-    outgoing, plane_in, held, line_in, line_all, plane_all, send, recv,
-):
-    y, x = lax.axis_index("lat"), lax.axis_index("lon")
-    plane = inner * lon_n
+    top = y == 0
+    bottom = y == lat_n - 1
+    depth, plane = lat_n // inner, inner * lon_n
+    chunk = chunk_a + chunk_b
+    piece = chunk // depth
     line = lax.div(y, inner)
     spot = lax.rem(y, inner) * lon_n + x
+    beside = []
+    for dy in (0, 1, -1):
+        for dx in offsets:
+            if dy or dx:
+                slot = [(-dx - other) % lon_n for other in offsets].index(0)
+                device = (lax.rem(y + dy + lat_n, lat_n), lax.rem(x + dx + lon_n, lon_n))
+                beside.append((device, 1 - dy, slot))
 
     def in_plane(step):
         other = lax.rem(spot + step, plane)
@@ -90,98 +85,37 @@
         other = lax.rem(line + step, depth)
         return other, (other * inner + lax.rem(y, inner), x)
 
+    greeted = [device for device, _, _ in beside]
+    greeted += [in_plane(step)[1] for step in range(1, plane)]
+    greeted += [in_line(step)[1] for step in range(1, depth)]
     barrier = pltpu.get_barrier_semaphore()
-    for step in range(1, plane):
-        pl.semaphore_signal(barrier, inc=1, device_id=in_plane(step)[1], device_id_type=MESH)
-    for step in range(1, depth):
-        pl.semaphore_signal(barrier, inc=1, device_id=in_line(step)[1], device_id_type=MESH)
-    for n in range(plane):
-        outgoing[n] = part[n * chunk : (n + 1) * chunk].astype(BF16)
-    pl.semaphore_wait(barrier, plane + depth - 2)
-
+    for device in greeted:
+        pl.semaphore_signal(barrier, inc=1, device_id=device, device_id_type=MESH)
     used = [0]
+
+    def push(source, target, device):
+        k = used[0]
+        used[0] += 1
+        copy = pltpu.make_async_remote_copy(
+            src_ref=source, dst_ref=target, send_sem=send.at[k], recv_sem=recv.at[k],
+            device_id=device, device_id_type=MESH,
+        )
+        copy.start()
+        return copy
 
     def exchange(count, where, source, target):
         copies = []
         for step in range(1, count):
             other, device = where(step)
-            k = used[0]
-            used[0] += 1
-            copy = pltpu.make_async_remote_copy(
-                src_ref=source(other),
-                dst_ref=target(step),
-                send_sem=send.at[k],
-                recv_sem=recv.at[k],
-                device_id=device,
-                device_id_type=MESH,
-            )
-            copy.start()
-            copies.append(copy)
-        for copy in copies:
-            copy.wait()
-
-    exchange(plane, in_plane, lambda o: outgoing.at[o], lambda step: plane_in.at[step - 1])
-    own = part[pl.ds(pl.multiple_of(spot * chunk, 8), chunk)]
-    for n in range(plane - 1):
-        own = own + plane_in[n].astype(F32)
-    for n in range(depth):
-        held[n] = own[n * piece : (n + 1) * piece]
-    exchange(depth, in_line, lambda o: held.at[o], lambda step: line_in.at[step - 1])
-    whole = held[line]
-    for n in range(depth - 1):
-        whole = whole + line_in[n]
-    line_all[line] = whole
-    exchange(depth, in_line, lambda o: line_all.at[line], lambda step: line_all.at[line])
-    plane_all[spot] = line_all[...].reshape(chunk, 128).astype(BF16)
-    exchange(plane, in_plane, lambda o: plane_all.at[spot], lambda step: plane_all.at[spot])
-
-    total = plane_all[...].reshape(plane * chunk, 128).astype(F32)
-    size = 1.0 / (9 * C * C)
-    second = [total[t * C : (t + 1) * C] for t in range(9)]
-    spots = total[9 * C : 10 * C]
-    tall = jnp.concatenate([lift[...].astype(F32).T] * 16, axis=0)
-    group = lax.broadcasted_iota(jnp.int32, (128, 128), 0) // 8
-    first = [
-        jnp.dot(
-            spots,
-            jnp.where(group == 4 * (t // 3) + t % 3, tall, 0.0),
-            precision=lax.Precision.HIGHEST,
-            preferred_element_type=F32,
-        )
-        for t in range(9)
-    ]
-    for blocks, ref in ((first, first_ref), (second, second_ref)):
-        squares = blocks[0] * blocks[0]
-        for t in range(1, 9):
-            squares = squares + blocks[t] * blocks[t]
-        factor = lax.rsqrt(jnp.sum(squares, keepdims=True) * size + 1e-06)
-        for t in range(9):
-            ref[:, t, :] = blocks[t] * factor
-
-
-def silu(v):
-    u = 0.5 * v
-    return u + u * jnp.tanh(u)
-
-
-def silu_slope(v):
-    sig = 0.5 + 0.5 * jnp.tanh(0.5 * v)
-    return sig * (1.0 + v * (1.0 - sig))
-
-
-def kernel(
-    rows, pairs, center,
-    table, index, blocks_in, taps, t_lift, s_lift, t_proj, s_proj,
-    tgt_ref, sum_ref,
-    x0, xa, xb, fld, u2, x4, dz4, slope1, slope2, dpre,
-    t_w1, t_w2, t_pr, s_w1, s_w2, s_pr, s_r, s_pt, joined, turned,
-):
-    total = rows + 2 * HALO
-    me = lax.axis_index("lat")
-    top = me == 0
-    bottom = me == lax.axis_size("lat") - 1
+            copies.append(push(source(other), target(step), device))
+        return copies
+
     base = index[0] * N_SCALARS
     sc = [table[base + k] for k in range(N_SCALARS)]
+    blocks_in[1, 0, 0:4] = clean[...] + sc[0] * noise[...]
+    blocks_in[1, 0, 4:8] = mean[...]
+    pl.semaphore_wait(barrier, len(greeted))
+    halos = [push(blocks_in.at[1, 0], blocks_in.at[sy, sx], device) for device, sy, sx in beside]
     lane = lax.broadcasted_iota(jnp.int32, (1, 1, 128), 2)
     lane_a = lane // 32
     lane_j = lane % 32 // 8
@@ -205,35 +139,6 @@
             return carry
 
         lax.fori_loop(0, count, step, 0)
-
-    cols = 2 * center
-    odd_lane = (lane_j[0] == 0) | (lane_j[0] == 2)
-    last_slot = blocks_in.shape[1] - 1
-    column = lax.broadcasted_iota(jnp.int32, (8, cols), 1)
-
-    def load_rows(slot, source, first, count):
-        def step(i, carry):
-            own = blocks_in[slot, 0, :, source + i, :]
-            beside = jnp.where(
-                column < SIDE,
-                blocks_in[slot, 1, :, source + i, :],
-                blocks_in[slot, last_slot, :, source + i, :],
-            )
-            turned[0:cols] = jnp.concatenate([own] * 16, axis=0).T
-            sides = jnp.concatenate([beside] * 16, axis=0).T
-            turned[cols : cols + SIDE] = sides[:SIDE]
-            turned[cols + SIDE : cols + 2 * SIDE] = sides[cols - SIDE :]
-            even = turned[pl.ds(0, pairs, stride=2)]
-            odd = turned[pl.ds(1, pairs, stride=2)]
-            x0[first + i] = jnp.where(odd_lane, odd, even)
-            return carry
-
-        lax.fori_loop(0, count, step, 0)
-
-    load_rows(0, rows - HALO, 0, HALO)
-    load_rows(1, 0, HALO, rows)
-    load_rows(2, 0, HALO + rows, HALO)
-    zero_edges(x0)
 
     def place(ref, t, block):
         a, b = divmod(t, 3)
@@ -245,7 +150,8 @@
         ref[...] = jnp.zeros_like(ref)
     none = jnp.zeros((8, C), BF16)
     four = jnp.zeros((4, C), F32)
-    lifts = [ref[...].astype(F32).T.astype(BF16) for ref in (t_lift, s_lift)]
+    lifts = [t_lift[...], s_lift[...]]
+    taps = [t_first, t_second, s_first, s_second]
     projs = [
         jnp.concatenate([ref[...].astype(F32), four], axis=0).astype(BF16)
         for ref in (t_proj, s_proj)
@@ -255,13 +161,13 @@
         for t in range(9):
             a, b = divmod(t, 3)
             mixed = lax.dot_general(
-                lifts[net], taps[2 * net, t], (((1,), (1,)), ((), ())),
+                lifts[net], taps[2 * net][t], (((1,), (1,)), ((), ())),
                 preferred_element_type=F32,
             )
             for side in range(2):
                 at = a * 32 + (b + side) * 8
                 joined[at : at + 8, side * C : (side + 1) * C] = mixed
-            place(w2, t, taps[2 * net + 1, t].T)
+            place(w2, t, taps[2 * net + 1][t].T)
         high = joined[...].astype(BF16)
         w1[0:128] = high
         w1[128:256] = (joined[...] - high.astype(F32)).astype(BF16)
@@ -285,7 +191,7 @@
         pr[0:C] = jnp.where(inside & jnp.logical_not(odd_slot), wide, 0.0).astype(BF16)
         pr[C : 2 * C] = jnp.where(inside & odd_slot, wide, 0.0).astype(BF16)
     for t in range(9):
-        place(s_r, t, taps[3, 8 - t])
+        place(s_r, t, taps[3][8 - t])
     s_pt[...] = jnp.zeros_like(s_pt)
     s_pt[40:56] = jnp.concatenate(
         [
@@ -294,6 +200,38 @@
         ],
         axis=0,
     )
+
+    for copy in halos:
+        copy.wait()
+
+    cols = 2 * center
+    odd_lane = (lane_j[0] == 0) | (lane_j[0] == 2)
+    last_slot = blocks_in.shape[1] - 1
+    column = lax.broadcasted_iota(jnp.int32, (8, cols), 1)
+
+    def load_rows(slot, source, first, count):
+        def step(i, carry):
+            own = blocks_in[slot, 0, :, source + i, :]
+            sides = jnp.where(
+                column < SIDE,
+                blocks_in[slot, 1, :, source + i, :],
+                blocks_in[slot, last_slot, :, source + i, :],
+            )
+            turned[0:cols] = jnp.concatenate([own] * 16, axis=0).T
+            sides = jnp.concatenate([sides] * 16, axis=0).T
+            turned[cols : cols + SIDE] = sides[:SIDE]
+            turned[cols + SIDE : cols + 2 * SIDE] = sides[cols - SIDE :]
+            even = turned[pl.ds(0, pairs, stride=2)]
+            odd = turned[pl.ds(1, pairs, stride=2)]
+            x0[first + i] = jnp.where(odd_lane, odd, even)
+            return carry
+
+        lax.fori_loop(0, count, step, 0)
+
+    load_rows(0, rows - HALO, 0, HALO)
+    load_rows(1, 0, HALO, rows)
+    load_rows(2, 0, HALO + rows, HALO)
+    zero_edges(x0)
 
     def spread(value, ref, r, nb):
         for n in range(nb):
@@ -439,9 +377,16 @@
         near = x4[pl.ds(HALO - 1 + a, rows), 0:center, :].reshape(cells, 512)
         grad = lax.dot_general(dz, near, dims, preferred_element_type=F32)
         for b in range(3):
-            sum_ref[3 * a + b] = (
+            at = (3 * a + b) * C
+            sum_a[at : at + C] = (
                 grad[:128, b * C : (b + 1) * C] + grad[128:, (b + 1) * C : (b + 2) * C]
             )
+    if plane * chunk_a > 9 * C:
+        sum_a[9 * C :] = jnp.zeros((plane * chunk_a - 9 * C, C), F32)
+        sum_b[C:] = jnp.zeros((plane * chunk_b - C, C), F32)
+    for n in range(plane):
+        out_a[n] = sum_a[n * chunk_a : (n + 1) * chunk_a].astype(BF16)
+    scatter_a = exchange(plane, in_plane, lambda o: out_a.at[o], lambda step: in_a.at[step - 1])
 
     def conv3(r):
         lhs = jnp.concatenate(
@@ -454,7 +399,64 @@
     d_before = dpre[:, 0:center, :].reshape(cells, 256)
     near = u2[middle, 0:center, :].reshape(cells, 128)
     grad = lax.dot_general(d_before, near, dims, preferred_element_type=F32)
-    sum_ref[9] = grad[:128] + pltpu.roll(grad[128:], 120, 1)
+    sum_b[0:C] = grad[:128] + pltpu.roll(grad[128:], 120, 1)
+    for n in range(plane):
+        out_b[n] = sum_b[n * chunk_b : (n + 1) * chunk_b].astype(BF16)
+    scatter_b = exchange(plane, in_plane, lambda o: out_b.at[o], lambda step: in_b.at[step - 1])
+
+    for copy in scatter_a:
+        copy.wait()
+    own_a = sum_a[pl.ds(pl.multiple_of(spot * chunk_a, 8), chunk_a)]
+    for n in range(plane - 1):
+        own_a = own_a + in_a[n].astype(F32)
+    for copy in scatter_b:
+        copy.wait()
+    own_b = sum_b[pl.ds(pl.multiple_of(spot * chunk_b, 8), chunk_b)]
+    for n in range(plane - 1):
+        own_b = own_b + in_b[n].astype(F32)
+    own = jnp.concatenate([own_a, own_b], axis=0)
+    for n in range(depth):
+        held[n] = own[n * piece : (n + 1) * piece]
+    for copy in exchange(
+        depth, in_line, lambda o: held.at[o], lambda step: line_in.at[step - 1]
+    ):
+        copy.wait()
+    whole = held[line]
+    for n in range(depth - 1):
+        whole = whole + line_in[n]
+    line_all[line] = whole
+    for copy in exchange(
+        depth, in_line, lambda o: line_all.at[line], lambda step: line_all.at[line]
+    ):
+        copy.wait()
+    plane_all[spot] = line_all[...].reshape(chunk, 128).astype(BF16)
+    for copy in exchange(
+        plane, in_plane, lambda o: plane_all.at[spot], lambda step: plane_all.at[spot]
+    ):
+        copy.wait()
+
+    size = 1.0 / (9 * C * C)
+    both = plane_all[:, 0:chunk_a].reshape(plane * chunk_a, 128).astype(F32)
+    spots = plane_all[:, chunk_a:chunk].reshape(plane * chunk_b, 128).astype(F32)[0:C]
+    second = [both[t * C : (t + 1) * C] for t in range(9)]
+    tall = jnp.concatenate([s_lift[...].astype(F32)] * 16, axis=0)
+    group = lax.broadcasted_iota(jnp.int32, (128, 128), 0) // 8
+    first = [
+        jnp.dot(
+            spots,
+            jnp.where(group == 4 * (t // 3) + t % 3, tall, 0.0),
+            precision=lax.Precision.HIGHEST,
+            preferred_element_type=F32,
+        )
+        for t in range(9)
+    ]
+    for parts, ref in ((first, first_ref), (second, second_ref)):
+        squares = parts[0] * parts[0]
+        for t in range(1, 9):
+            squares = squares + parts[t] * parts[t]
+        factor = lax.rsqrt(jnp.sum(squares, keepdims=True) * size + 1e-06)
+        for t in range(9):
+            ref[t] = parts[t] * factor
 
 
 def local(
@@ -471,29 +473,26 @@
 
     offsets = [0, 1] if lon_n == 2 else [0, 1, -1]
     slots = len(offsets)
-    links = 3 * slots - 1
-    blocks = pl.pallas_call(
-        functools.partial(halo_kernel, lat_n, lon_n, offsets),
-        out_shape=jax.ShapeDtypeStruct((3, slots, 8, rows, cols), F32),
-        in_specs=[smem, smem, vmem, vmem, vmem],
-        out_specs=vmem,
-        scratch_shapes=[pltpu.SemaphoreType.DMA((links,)), pltpu.SemaphoreType.DMA((links,))],
-        compiler_params=pltpu.CompilerParams(
-            collective_id=0, has_side_effects=True, vmem_limit_bytes=16 * 1024 * 1024
+    inner = 4 if lat_n % 4 == 0 else 1
+    depth, plane = lat_n // inner, inner * lon_n
+    chunk_a = -(-9 * C // (plane * 16)) * 16
+    chunk_b = -(-C // (plane * 16)) * 16
+    while (chunk_a + chunk_b) % (8 * depth):
+        chunk_b += 16
+    chunk = chunk_a + chunk_b
+    piece = chunk // depth
+    links = 3 * slots - 1 + 3 * (plane - 1) + 2 * (depth - 1)
+    target, first, second = pl.pallas_call(
+        functools.partial(
+            kernel, rows, pairs, center, lat_n, lon_n, offsets, inner, chunk_a, chunk_b
         ),
-    )(table, sigma_index, clean, noise, mean_field)
-
-    taps = jnp.stack(
-        [teacher_first, teacher_second, student_first, student_second]
-    ).transpose(0, 2, 1, 3)
-    target, sums = pl.pallas_call(
-        functools.partial(kernel, rows, pairs, center),
         out_shape=[
             jax.ShapeDtypeStruct((4, rows, cols), F32),
-            jax.ShapeDtypeStruct((10, C, C), F32),
+            jax.ShapeDtypeStruct((9, C, C), F32),
+            jax.ShapeDtypeStruct((9, C, C), F32),
         ],
-        in_specs=[smem, smem] + [vmem] * 6,
-        out_specs=[vmem] * 2,
+        in_specs=[smem, smem] + [vmem] * 11,
+        out_specs=[vmem] * 3,
         scratch_shapes=[pltpu.VMEM((total, pairs, 128), F32)] * 4
         + [
             pltpu.VMEM((total, pairs, 128), BF16),
@@ -514,31 +513,13 @@
             pltpu.VMEM((C, 2 * C), BF16),
             pltpu.VMEM((C, 2 * C), F32),
             pltpu.VMEM((2 * pairs, 128), F32),
-        ],
-        compiler_params=pltpu.CompilerParams(vmem_limit_bytes=56 * 1024 * 1024),
-    )(
-        table, sigma_index, blocks, taps,
-        teacher_lift, student_lift, teacher_proj, student_proj,
-    )
-
-    inner = 4 if lat_n % 4 == 0 else 1
-    depth, plane = lat_n // inner, inner * lon_n
-    piece = -(-10 * C // (plane * depth * 8)) * 8
-    while piece * depth % 16:
-        piece += 8
-    chunk = piece * depth
-    part = sums.reshape(10 * C, C)
-    if plane * chunk > 10 * C:
-        part = jnp.pad(part, ((0, plane * chunk - 10 * C), (0, 0)))
-    links = 2 * (plane + depth - 2)
-    update_first, update_second = pl.pallas_call(
-        functools.partial(sum_kernel, inner, depth, lon_n, chunk, piece),
-        out_shape=[jax.ShapeDtypeStruct((C, 9, C), F32)] * 2,
-        in_specs=[vmem] * 2,
-        out_specs=[vmem] * 2,
-        scratch_shapes=[
-            pltpu.VMEM((plane, chunk, 128), BF16),
-            pltpu.VMEM((plane - 1, chunk, 128), BF16),
+            pltpu.VMEM((3, slots, 8, rows, cols), F32),
+            pltpu.VMEM((plane * chunk_a, 128), F32),
+            pltpu.VMEM((plane * chunk_b, 128), F32),
+            pltpu.VMEM((plane, chunk_a, 128), BF16),
+            pltpu.VMEM((plane, chunk_b, 128), BF16),
+            pltpu.VMEM((plane - 1, chunk_a, 128), BF16),
+            pltpu.VMEM((plane - 1, chunk_b, 128), BF16),
             pltpu.VMEM((depth, piece, 128), F32),
             pltpu.VMEM((depth - 1, piece, 128), F32),
             pltpu.VMEM((depth, piece, 128), F32),
@@ -547,10 +528,17 @@
             pltpu.SemaphoreType.DMA((links,)),
         ],
         compiler_params=pltpu.CompilerParams(
-            collective_id=1, has_side_effects=True, vmem_limit_bytes=32 * 1024 * 1024
+            collective_id=0, has_side_effects=True, vmem_limit_bytes=56 * 1024 * 1024
         ),
-    )(part, student_lift)
-    return (target, update_first, update_second)
+    )(
+        table, sigma_index, clean, noise, mean_field,
+        *(
+            taps.transpose(1, 0, 2)
+            for taps in (teacher_first, teacher_second, student_first, student_second)
+        ),
+        teacher_lift.T, student_lift.T, teacher_proj, student_proj,
+    )
+    return (target, first.transpose(1, 0, 2), second.transpose(1, 0, 2))
 
 
 def solution(mesh):

time: 83.4 us -> 70.9 us (0.85)
  local copies, waits for them, and re-layouts: 9.58 us -> 4.17 us
  Pallas kernels: 69.6 us -> 65.2 us
  other arithmetic: 2.41 us -> 0 us
    unnamed x18 -> x5, local copies, waits for them, and re-layouts: 9.58 us -> 4.17 us
    pallas_call x3 -> x1, Pallas kernels: 69.6 us -> 65.2 us  [local(): pl.pallas_call(functools.partial(kernel, rows, pairs, center, lat_n, lon_...]
    transpose x1 -> x0, other arithmetic: 2.41 us -> none  [local(): taps = jnp.stack([teacher_first, teacher_second, student_first, student_s...]
where the time goes in v3:
time: 70.9 us; the launch traced here: 70.7 us
  Pallas kernels  65.2 us (92%)
  local copies, waits for them, and re-layouts  4.17 us (6%)
  between operations  1.29 us (2%)
    pallas_call x1, Pallas kernels, local(): pl.pallas_call(functools.partial(kernel, rows, pairs, center, lat_n, lon_...  65.2 us
    unnamed x5, local copies, waits for them, and re-layouts  4.17 us

profile of v3, /device:TPU:0, one launch (start us, length us, event | category | flops | bytes accessed | tf_op | source)
XLA Modules:
  0.0 70.7 jit_solution(6518295803221529584)
XLA Ops:
  1.3 65.2 %shard_map.148 = (f32[4,16,128]{2,1,0:T(8,128)}, f32[9,128,128]{2,1,0:T(8,128)}, f32[9,128,128]{2,1,0:T(8,128)}) custom-call(f32[368]{0:T(512)} %constant.2.clone.table, s32[1]{0:T(128)S(6)} %copy.19.index, f32[4,16,128]{2,1,0:T(8,128)} %clean.1, f32[4,16,128]{2,1,0:T(8,128)} %noise.1, f32[4,16,128]{2,1,0:T(8,128)} %mean.1, bf16[9,128,128]{2,1,0:T(8,128)(2,1)} %bitcast.10, ...), custom_call_target="tpu_custom_call" | custom-call | tf_op jit(solution)/shard_map/pallas_call | solution.py:485
  66.5 1.4 %copy.20 = f32[4,16,128]{2,1,0:T(8,128)} copy(f32[4,16,128]{2,1,0:T(8,128)} %get-tuple-element.12) | data formatting | bytes 65536
  67.9 0.0 copy-start
  67.9 2.0 %copy.21 = f32[128,9,128]{2,0,1:T(8,128)} copy(f32[128,9,128]{2,0,1:T(8,128)} %bitcast.9) | data formatting | bytes 1179648
  69.9 0.0 copy-done
  69.9 0.8 %copy.22 = f32[128,9,128]{2,0,1:T(8,128)} copy(f32[128,9,128]{2,0,1:T(8,128)S(1)} %bitcast.8) | data formatting | bytes 1179648
Async XLA Ops:
  67.9 2.0 %copy-start = (f32[9,128,128]{2,1,0:T(8,128)S(1)}, f32[9,128,128]{2,1,0:T(8,128)}, u32[]{:S(2)}) copy-start(f32[9,128,128]{2,1,0:T(8,128)} %get-tuple-element.8) | copy-start | bytes 1769476

commit v4 on v3

--- a/solution.py
+++ b/solution.py
@@ -38,6 +38,10 @@
 
 N_SCALARS = 23
 MESH = pl.DeviceIdType.MESH
+
+
+def even_block(count, largest):
+    return max(n for n in range(1, largest + 1) if count % n == 0)
 
 
 def silu(v):
@@ -201,9 +205,6 @@
         axis=0,
     )
 
-    for copy in halos:
-        copy.wait()
-
     cols = 2 * center
     odd_lane = (lane_j[0] == 0) | (lane_j[0] == 2)
     last_slot = blocks_in.shape[1] - 1
@@ -228,8 +229,15 @@
 
         lax.fori_loop(0, count, step, 0)
 
+    slots = len(offsets)
+    for copy in halos[: slots - 1]:
+        copy.wait()
+    load_rows(1, 0, HALO, rows)
+    for copy in halos[slots - 1 : 2 * slots - 1]:
+        copy.wait()
     load_rows(0, rows - HALO, 0, HALO)
-    load_rows(1, 0, HALO, rows)
+    for copy in halos[2 * slots - 1 :]:
+        copy.wait()
     load_rows(2, 0, HALO + rows, HALO)
     zero_edges(x0)
 
@@ -303,15 +311,17 @@
 
     def teacher(state, level, first):
         last = total - first
-        conv1(state, q_inv[level], t_w1, first, last, 8, False)
-        conv2(t_w2, t_pr, first + 1, last - 1, 6, False)
+        conv1(state, q_inv[level], t_w1, first, last, even_block(last - first, 10), False)
+        conv2(t_w2, t_pr, first + 1, last - 1, even_block(last - first - 2, 13), False)
 
     def update(dst, first, fn):
+        size = even_block(total - 2 * first, 6)
+
         def body(r):
-            at = pl.ds(r, 2)
+            at = pl.ds(r, size)
             dst[at] = fn(at)
 
-        blocks(first, total - first, 2, body)
+        blocks(first, total - first, size, body)
 
     def euler(src, dst, first, level, ratio):
         cx = jnp.where(is_x, 1.0 + ratio * rest[level], 1.0)
@@ -353,20 +363,22 @@
         for i in range(count):
             tgt_ref[:, first + i, :] = flat[8 * i : 8 * i + 4]
 
-    conv1(x0, q_inv[0], s_w1, 7, total - 7, 4, True)
-    conv2(s_w2, s_pr, 8, total - 8, 6, True)
+    conv1(x0, q_inv[0], s_w1, 7, total - 7, even_block(total - 14, 5), True)
+    conv2(s_w2, s_pr, 8, total - 8, even_block(total - 16, 9), True)
+
+    step_rows = even_block(total - 16, 6)
 
     def backward(r):
-        at = pl.ds(r, 2)
+        at = pl.ds(r, step_rows)
         d_field = jnp.where(
             is_x, pull * (keep[0] * x0[at] + gain[0] * fld[at] - xa[at]), 0.0
         ).astype(BF16)
         d_gated = jnp.dot(
-            d_field.reshape(2 * pairs, 128), s_pt[...], preferred_element_type=F32
-        ).reshape(2, pairs, 256)
-        spread(d_gated * slope2[at], dz4, r, 2)
-
-    blocks(8, total - 8, 2, backward)
+            d_field.reshape(step_rows * pairs, 128), s_pt[...], preferred_element_type=F32
+        ).reshape(step_rows, pairs, 256)
+        spread(d_gated * slope2[at], dz4, r, step_rows)
+
+    blocks(8, total - 8, step_rows, backward)
     zero_edges(dz4)
 
     cells = rows * center
@@ -388,14 +400,18 @@
         out_a[n] = sum_a[n * chunk_a : (n + 1) * chunk_a].astype(BF16)
     scatter_a = exchange(plane, in_plane, lambda o: out_a.at[o], lambda step: in_a.at[step - 1])
 
+    conv_rows = even_block(rows, 8)
+
     def conv3(r):
         lhs = jnp.concatenate(
-            [dz4[pl.ds(r + a - 1, 4)].reshape(4 * pairs, 512) for a in range(3)], axis=1
-        )
-        dh = jnp.dot(lhs, s_r[...], preferred_element_type=F32).reshape(4, pairs, 256)
-        dpre[pl.ds(r - HALO, 4)] = (dh * slope1[pl.ds(r, 4)]).astype(BF16)
-
-    blocks(HALO, HALO + rows, 4, conv3)
+            [dz4[pl.ds(r + a - 1, conv_rows)].reshape(conv_rows * pairs, 512) for a in range(3)], axis=1
+        )
+        dh = jnp.dot(lhs, s_r[...], preferred_element_type=F32).reshape(
+            conv_rows, pairs, 256
+        )
+        dpre[pl.ds(r - HALO, conv_rows)] = (dh * slope1[pl.ds(r, conv_rows)]).astype(BF16)
+
+    blocks(HALO, HALO + rows, conv_rows, conv3)
     d_before = dpre[:, 0:center, :].reshape(cells, 256)
     near = u2[middle, 0:center, :].reshape(cells, 128)
     grad = lax.dot_general(d_before, near, dims, preferred_element_type=F32)

time: 70.9 us -> 64.8 us (0.914)
  Pallas kernels: 65.2 us -> 59.1 us
    pallas_call x1, Pallas kernels: 65.2 us -> 59.1 us  [local(): pl.pallas_call(functools.partial(kernel, rows, pairs, center, lat_n, lon_...]
where the time goes in v4:
time: 64.8 us; the launch traced here: 64.6 us
  Pallas kernels  59.1 us (91%)
  local copies, waits for them, and re-layouts  4.17 us (6%)
  between operations  1.29 us (2%)
    pallas_call x1, Pallas kernels, local(): pl.pallas_call(functools.partial(kernel, rows, pairs, center, lat_n, lon_...  59.1 us
    unnamed x5, local copies, waits for them, and re-layouts  4.17 us

profile of v4, /device:TPU:0, one launch (start us, length us, event | category | flops | bytes accessed | tf_op | source)
XLA Modules:
  0.0 64.6 jit_solution(14723090827039530883)
XLA Ops:
  1.3 59.1 %shard_map.148 = (f32[4,16,128]{2,1,0:T(8,128)}, f32[9,128,128]{2,1,0:T(8,128)}, f32[9,128,128]{2,1,0:T(8,128)}) custom-call(f32[368]{0:T(512)} %constant.2.clone.table, s32[1]{0:T(128)S(6)} %copy.19.index, f32[4,16,128]{2,1,0:T(8,128)} %clean.1, f32[4,16,128]{2,1,0:T(8,128)} %noise.1, f32[4,16,128]{2,1,0:T(8,128)} %mean.1, bf16[9,128,128]{2,1,0:T(8,128)(2,1)} %bitcast.10, ...), custom_call_target="tpu_custom_call" | custom-call | tf_op jit(solution)/shard_map/pallas_call | solution.py:501
  60.4 1.4 %copy.20 = f32[4,16,128]{2,1,0:T(8,128)} copy(f32[4,16,128]{2,1,0:T(8,128)} %get-tuple-element.12) | data formatting | bytes 65536
  61.8 0.0 copy-start
  61.8 2.0 %copy.21 = f32[128,9,128]{2,0,1:T(8,128)} copy(f32[128,9,128]{2,0,1:T(8,128)} %bitcast.9) | data formatting | bytes 1179648
  63.7 0.0 copy-done
  63.8 0.8 %copy.22 = f32[128,9,128]{2,0,1:T(8,128)} copy(f32[128,9,128]{2,0,1:T(8,128)S(1)} %bitcast.8) | data formatting | bytes 1179648
Async XLA Ops:
  61.8 2.0 %copy-start = (f32[9,128,128]{2,1,0:T(8,128)S(1)}, f32[9,128,128]{2,1,0:T(8,128)}, u32[]{:S(2)}) copy-start(f32[9,128,128]{2,1,0:T(8,128)} %get-tuple-element.8) | copy-start | bytes 1769476

commit v5 on v4

--- a/solution.py
+++ b/solution.py
@@ -311,11 +311,11 @@
 
     def teacher(state, level, first):
         last = total - first
-        conv1(state, q_inv[level], t_w1, first, last, even_block(last - first, 10), False)
-        conv2(t_w2, t_pr, first + 1, last - 1, even_block(last - first - 2, 13), False)
+        conv1(state, q_inv[level], t_w1, first, last, even_block(last - first, 16), False)
+        conv2(t_w2, t_pr, first + 1, last - 1, even_block(last - first - 2, 15), False)
 
     def update(dst, first, fn):
-        size = even_block(total - 2 * first, 6)
+        size = even_block(total - 2 * first, 10)
 
         def body(r):
             at = pl.ds(r, size)
@@ -363,10 +363,10 @@
         for i in range(count):
             tgt_ref[:, first + i, :] = flat[8 * i : 8 * i + 4]
 
-    conv1(x0, q_inv[0], s_w1, 7, total - 7, even_block(total - 14, 5), True)
+    conv1(x0, q_inv[0], s_w1, 7, total - 7, even_block(total - 14, 10), True)
     conv2(s_w2, s_pr, 8, total - 8, even_block(total - 16, 9), True)
 
-    step_rows = even_block(total - 16, 6)
+    step_rows = even_block(total - 16, 9)
 
     def backward(r):
         at = pl.ds(r, step_rows)
@@ -400,7 +400,7 @@
         out_a[n] = sum_a[n * chunk_a : (n + 1) * chunk_a].astype(BF16)
     scatter_a = exchange(plane, in_plane, lambda o: out_a.at[o], lambda step: in_a.at[step - 1])
 
-    conv_rows = even_block(rows, 8)
+    conv_rows = even_block(rows, 16)
 
     def conv3(r):
         lhs = jnp.concatenate(

time: 64.8 us -> 64.6 us (level)
  no operation moved by 1% of the time
where the time goes in v5:
time: 64.6 us; the launch traced here: 64.4 us
  Pallas kernels  58.9 us (91%)
  local copies, waits for them, and re-layouts  4.17 us (6%)
  between operations  1.29 us (2%)
    pallas_call x1, Pallas kernels, local(): pl.pallas_call(functools.partial(kernel, rows, pairs, center, lat_n, lon_...  58.9 us
    unnamed x5, local copies, waits for them, and re-layouts  4.17 us

profile of v5, /device:TPU:0, one launch (start us, length us, event | category | flops | bytes accessed | tf_op | source)
XLA Modules:
  0.0 64.4 jit_solution(10433335348573189850)
XLA Ops:
  1.3 58.9 %shard_map.148 = (f32[4,16,128]{2,1,0:T(8,128)}, f32[9,128,128]{2,1,0:T(8,128)}, f32[9,128,128]{2,1,0:T(8,128)}) custom-call(f32[368]{0:T(512)} %constant.2.clone.table, s32[1]{0:T(128)S(6)} %copy.19.index, f32[4,16,128]{2,1,0:T(8,128)} %clean.1, f32[4,16,128]{2,1,0:T(8,128)} %noise.1, f32[4,16,128]{2,1,0:T(8,128)} %mean.1, bf16[9,128,128]{2,1,0:T(8,128)(2,1)} %bitcast.10, ...), custom_call_target="tpu_custom_call" | custom-call | tf_op jit(solution)/shard_map/pallas_call | solution.py:501
  60.2 1.4 %copy.20 = f32[4,16,128]{2,1,0:T(8,128)} copy(f32[4,16,128]{2,1,0:T(8,128)} %get-tuple-element.12) | data formatting | bytes 65536
  61.6 0.0 copy-start
  61.6 2.0 %copy.21 = f32[128,9,128]{2,0,1:T(8,128)} copy(f32[128,9,128]{2,0,1:T(8,128)} %bitcast.9) | data formatting | bytes 1179648
  63.5 0.0 copy-done
  63.5 0.8 %copy.22 = f32[128,9,128]{2,0,1:T(8,128)} copy(f32[128,9,128]{2,0,1:T(8,128)S(1)} %bitcast.8) | data formatting | bytes 1179648
Async XLA Ops:
  61.6 2.0 %copy-start = (f32[9,128,128]{2,1,0:T(8,128)S(1)}, f32[9,128,128]{2,1,0:T(8,128)}, u32[]{:S(2)}) copy-start(f32[9,128,128]{2,1,0:T(8,128)} %get-tuple-element.8) | copy-start | bytes 1769476
